TPU v7x, 128 devices: a whole 4x4x4 slice. The times are simulated.
128 devices in a mesh: rows: 8 (over x_hi, y), seq: 16 (over z, x_lo, core).
Axes of the slice: x: 4 (x_hi: 2, x_lo: 2; x = x_hi * 2 + x_lo), y: 4, z: 4, core: 2. Of those that a mesh axis runs over, the one named last changes fastest.
Arguments:
- hidden_in: bfloat16 [16, 1024, 1024], P('rows', 'seq'), may hold values from -6 to 6
- query_weight: bfloat16 [1024, 2048], replicated, may hold values from -0.1875 to 0.1875
- key_weight: bfloat16 [1024, 1024], replicated, may hold values from -0.1875 to 0.1875
- value_weight: bfloat16 [1024, 1024], replicated, may hold values from -0.1875 to 0.1875
- output_weight: bfloat16 [1024, 2048], replicated, may hold values from -0.5 to 0.5
- gate_weight: bfloat16 [1024, 3072], replicated, may hold values from -0.1875 to 0.1875
- up_weight: bfloat16 [1024, 3072], replicated, may hold values from -0.1875 to 0.1875
- down_weight: bfloat16 [1024, 3072], replicated, may hold values from -0.109375 to 0.109375
- query_gain: float32 [128], replicated, may hold values from 1.2 to 2.4
- key_gain: float32 [128], replicated, may hold values from 0.1 to 1.9
- attention_gain: float32 [1024], replicated, may hold values from 0.1 to 1.9
- feedforward_gain: float32 [1024], replicated, may hold values from 0.1 to 1.9
- document_ids: int32 [16, 1024], P('rows', 'seq'), may hold values from 0 to 8, as said below
- cotangent: bfloat16 [16, 1024, 1024], P('rows', 'seq'), may hold values from -6 to 6
Outputs:
- layer_output: float32 [16, 1024, 1024], P('rows', 'seq')
- input_grad: float32 [16, 1024, 1024], P('rows', 'seq')
- query_weight_grad: float32 [1024, 2048], P('seq')
- key_weight_grad: float32 [1024, 1024], P('seq')
- value_weight_grad: float32 [1024, 1024], P('seq')
- output_weight_grad: float32 [1024, 2048], P('seq')
- gate_weight_grad: float32 [1024, 3072], P('seq')
- up_weight_grad: float32 [1024, 3072], P('seq')
- down_weight_grad: float32 [1024, 3072], P('seq')
- query_gain_grad: float32 [128], replicated
- key_gain_grad: float32 [128], replicated
- attention_gain_grad: float32 [1024], replicated
- feedforward_gain_grad: float32 [1024], replicated
Inputs may be any that keep to these rules, and one draw needn't show every extreme that they name: `document_ids`: along each row the ids start at 0 and never fall.
All inputs are finite; a program needn't handle non-finite values.
Results may differ from a plain program's by a relative error of at most 0.035.
Values may be sent and summed in bfloat16 or wider, within the bound.
A program may use at most 192 MiB of HBM per device.

v0:
```python
import functools

import jax
import jax.numpy as jnp
import numpy as np
from jax import lax
from jax.experimental import pallas as pl
from jax.experimental.pallas import tpu as pltpu
from jax.sharding import PartitionSpec as P

HD = 128
EPSILON = 1e-06
ROPE_BASE = 1000000.0
MASKED = -1e30
LOG2E = 1.4426950408889634
SCALE = HD ** (-0.5)
MESH = pl.DeviceIdType.MESH
F32 = jnp.float32
BF16 = jnp.bfloat16

YS = 4
ZS = 4
XS = 4


def place():
    rows, seq = lax.axis_index("rows"), lax.axis_index("seq")
    return (rows // YS, rows % YS, seq // 4, (seq // 2) % 2, seq % 2)


def device(xh, y, z, xl, c):
    return (xh * YS + y, z * 4 + xl * 2 + c)


def shifted(at, dx=0, dy=0, dz=0, dc=0, flip_xl=0, flip_xh=0):
    xh, y, z, xl, c = at
    if dx:
        x = (xh * 2 + xl + dx) % XS
        xh, xl = x // 2, x % 2
    if flip_xl:
        xl = 1 - xl
    if flip_xh:
        xh = 1 - xh
    if dc:
        c = 1 - c
    return (xh, (y + dy) % YS, (z + dz) % ZS, xl, c)


class Landing:
    def __init__(self, copy):
        self.copy, self.here = copy, False

    def arrive(self):
        if not self.here:
            self.copy.wait_recv()
            self.here = True


class Net:
    def __init__(self, send_sems, recv_sems, local_sems):
        self.send_sems, self.recv_sems, self.local_sems = send_sems, recv_sems, local_sems
        self.sent, self.kept = [], 0

    def barrier(self, targets):
        barrier = pltpu.get_barrier_semaphore()
        for target in targets:
            pl.semaphore_signal(barrier, inc=1, device_id=device(*target), device_id_type=MESH)
        pl.semaphore_wait(barrier, len(targets))

    def send(self, src, dst, target):
        i = len(self.sent)
        copy = pltpu.make_async_remote_copy(
            src_ref=src,
            dst_ref=dst,
            send_sem=self.send_sems.at[i],
            recv_sem=self.recv_sems.at[i],
            device_id=device(*target),
            device_id_type=MESH,
        )
        copy.start()
        self.sent.append(Landing(copy))
        return self.sent[-1]

    def keep(self, src, dst):
        copy = pltpu.make_async_copy(src, dst, self.local_sems.at[self.kept])
        self.kept += 1
        copy.start()
        return copy

    def drain(self):
        for landing in self.sent:
            landing.arrive()
            landing.copy.wait_send()


def shape(dims, dtype=BF16):
    return jax.ShapeDtypeStruct(dims, dtype)


ZC = [(dz, dc) for dz in range(ZS) for dc in range(2) if (dz, dc) != (0, 0)]
ORDER = (0, 1, 3, 2)
BLOCK = 256
SENDS = 188
KEEPS = 64


def rope_tables():
    half = HD // 2
    frequency = ROPE_BASE ** (-(np.arange(half, dtype=np.float64) * 2.0 / HD))
    angles = np.arange(1024, dtype=np.float64)[:, None] * frequency[None, :]
    cosines = np.concatenate([np.cos(angles)] * 2, axis=1)
    sines = np.concatenate([-np.sin(angles), np.sin(angles)], axis=1)
    return (cosines.astype(np.float32), sines.astype(np.float32))


def dot_nn(left, right):
    return jnp.dot(left, right, preferred_element_type=F32)


def dot_nt(left, right):
    return lax.dot_general(left, right, (((1,), (1,)), ((), ())), preferred_element_type=F32)


def dot_tn(left, right):
    return lax.dot_general(left, right, (((0,), (0,)), ((), ())), preferred_element_type=F32)


def normalize(vector, scales):
    inverse = lax.rsqrt(jnp.mean(vector * vector, axis=-1, keepdims=True) + EPSILON)
    return (vector * inverse * scales, inverse)


def norm_back(gradient, vector, inverse, scales):
    normed = vector * inverse
    scales_grad = jnp.sum(gradient * normed, axis=0, keepdims=True)
    scaled = gradient * scales
    vector_grad = inverse * (scaled - normed * jnp.mean(scaled * normed, axis=-1, keepdims=True))
    return (vector_grad, scales_grad)


def aligned(index, width):
    return pl.ds(pl.multiple_of(index * width, width), width)


class Refs:
    pass


INPUTS = (
    "hidden", "cotangent", "documents",
    "query_weight", "key_weight", "value_weight", "output_weight", "gate_weight", "up_weight", "down_weight",
    "cosines", "sines", "query_gain", "key_gain", "attention_gain", "feedforward_gain",
)
IN_VMEM = ("cosines", "sines", "query_gain", "key_gain", "attention_gain", "feedforward_gain")
OUTPUTS = (
    ("out", (2, 64, 1024), F32),
    ("grad", (2, 64, 1024), F32),
    ("wide", (2, 64, 2048), BF16),
    ("narrow", (2, 64, 1024), BF16),
    ("gate_up_grad", (2, 64, 3072), BF16),
    ("down_grad", (64, 3072), BF16),
    ("gains", (24, 128), F32),
    ("residual_all", (1024, 1024), BF16),
    ("gate_up_all", (1024, 768), BF16),
    ("down_all", (1024, 1024), BF16),
    ("activated_all", (1024, 384), BF16),
)
SCRATCH = (
    ("head_weights", (1024, 512), BF16),
    ("wo", (1024, 2048), BF16),
    ("wgu", (1024, 6144), BF16),
    ("wd", (1024, 3072), BF16),
    ("row", (4, 2, 2, 64, 1024), BF16),
    ("upstream", (2, 64, 1024), BF16),
    ("row_documents", (4, 2, 2, 8, 128), F32),
    ("document_column", (1024, 128), F32),
    ("raw", (1024, 384), F32),
    ("inverses", (1024, 3), F32),
    ("queries", (1024, 256), BF16),
    ("keys", (1024, 128), BF16),
    ("values", (1024, 128), BF16),
    ("attended", (1024, 256), F32),
    ("attn_heads", (4, 2, 2, 64, 256), BF16),
    ("log_total", (1024, 2), F32),
    ("attn_tokens", (2, 64, 2048), BF16),
    ("branch", (128, 1024), F32),
    ("residual", (128, 1024), F32),
    ("residual_low", (128, 1024), BF16),
    ("gate_factor", (128, 3072), F32),
    ("up_factor", (128, 3072), F32),
    ("activated", (128, 3072), BF16),
    ("layer_output", (2, 64, 1024), F32),
    ("down_low", (128, 1024), BF16),
    ("gate_up_low", (128, 6144), BF16),
    ("residual_grad", (128, 1024), F32),
    ("branch_low", (2, 64, 1024), BF16),
    ("attn_grad", (2, 64, 2048), BF16),
    ("attn_grad_row", (4, 2, 2, 64, 256), BF16),
    ("branch_row", (4, 2, 2, 64, 1024), BF16),
    ("lows", (4, 2, 2, 64, 512), BF16),
    ("key_sum", (1024, 128), F32),
    ("value_sum", (1024, 128), F32),
    ("low_tokens", (2, 64, 4096), BF16),
    ("input_grad", (2, 64, 1024), F32),
    ("own_a", (4, 2, 2, 4, 16, 768), BF16),
    ("own_b", (4, 2, 2, 64, 768), BF16),
    ("own_c", (4, 2, 2, 4, 16, 384), BF16),
    ("all_a", (3, 4, 2, 2, 16, 768), BF16),
    ("all_b", (3, 4, 2, 64, 384), BF16),
    ("all_c", (3, 2, 2, 4, 16, 384), BF16),
    ("next_a", (4, 2, 2, 16, 768), BF16),
    ("next_b", (4, 2, 64, 384), BF16),
    ("next_c", (2, 2, 4, 16, 384), BF16),
    ("then_a", (3, 4, 2, 16, 384), BF16),
    ("then_b", (3, 2, 64, 384), BF16),
    ("then_c", (3, 2, 2, 16, 384), BF16),
    ("done_a", (4, 2, 16, 384), BF16),
    ("done_b", (2, 64, 384), BF16),
    ("done_c", (2, 2, 16, 384), BF16),
    ("got_wide", (16, 2048), BF16),
    ("got_narrow", (16, 1024), BF16),
    ("got_b", (64, 768), BF16),
    ("got_c", (16, 1536), BF16),
    ("gains_own", (24, 128), F32),
    ("gains_next", (24, 128), F32),
    ("gains_last", (24, 128), F32),
    ("gains_final", (24, 128), F32),
    ("gains_y", (3, 24, 128), F32),
    ("gains_x", (3, 24, 128), F32),
    ("gains_zc", (7, 24, 128), F32),
)


def layer_kernel(*refs):
    names = INPUTS + tuple(n for n, _, _ in OUTPUTS) + tuple(n for n, _, _ in SCRATCH)
    r = Refs()
    for name, ref in zip(names, refs):
        setattr(r, name, ref)
    net = Net(*refs[len(names) :])
    at = place()
    xh, y, z, xl, c = at
    x = xh * 2 + xl
    head = z * 2 + c
    sibling = shifted(at, dc=1)
    partner = shifted(at, flip_xl=1)
    seq_others = [
        shifted(at, dz=dz, dc=dc, flip_xl=dx)
        for dz in range(ZS)
        for dx in range(2)
        for dc in range(2)
        if (dz, dx, dc) != (0, 0, 0)
    ]
    zc = [shifted(at, dz=dz, dc=dc) for dz, dc in ZC]
    yc = [shifted(at, dy=dy, dc=dc) for dy, dc in ZC]
    xc = [shifted(at, dx=dx, dc=dc) for dx, dc in ZC]
    ys = [shifted(at, dy=step) for step in range(1, 4)]
    xs = [shifted(at, dx=step) for step in range(1, 4)]
    zs = [shifted(at, dz=step) for step in range(1, 4)]
    replicas = [
        shifted(at, dy=dy, flip_xh=dx) for dy in range(YS) for dx in range(2) if (dy, dx) != (0, 0)
    ]

    loads = [
        net.keep(ref.at[:, aligned(head, width)], r.head_weights.at[:, pl.ds(start, width)])
        for ref, start, width in (
            (r.query_weight, 0, 256),
            (r.key_weight, 256, 128),
            (r.value_weight, 384, 128),
        )
    ]
    load_wo = net.keep(r.output_weight, r.wo)
    load_wgu = [
        net.keep(r.gate_weight, r.wgu.at[:, pl.ds(0, 3072)]),
        net.keep(r.up_weight, r.wgu.at[:, pl.ds(3072, 3072)]),
    ]
    load_wd = net.keep(r.down_weight, r.wd)

    barrier_targets = list(seq_others) + yc[1:] + xc[1:] + replicas
    net.barrier(barrier_targets)
    direct = {}
    for dz in (0, 1, 3, 2):
        for dx in range(2):
            if (dz, dx) != (0, 0):
                target = shifted(at, dz=dz, flip_xl=dx)
                direct[dz, dx] = net.send(r.hidden.at[target[3]], r.row.at[z, xl, c], target)
    own_block = net.keep(r.hidden.at[xl], r.row.at[z, xl, c])
    document_landings = [
        net.send(r.documents.at[t[3]], r.row_documents.at[z, xl, c], t) for t in seq_others
    ]
    document_landings_own = net.keep(r.documents.at[xl], r.row_documents.at[z, xl, c])
    upstream_landing = net.send(r.cotangent.at[1 - xl], r.upstream.at[xl], partner)
    upstream_own = net.keep(r.cotangent.at[xl], r.upstream.at[xl])

    forwarded = {}

    def forward_blocks(dz):
        source = (z - dz) % ZS
        for dx in range(2):
            if (dz, dx) == (0, 0):
                own_block.wait()
            else:
                direct[dz, dx].arrive()
            block = r.row.at[source, (xl + dx) % 2, c]
            forwarded[dz, dx] = net.send(block, block, sibling)

    def project(dz):
        source = (z - dz) % ZS
        for dx in range(2):
            forwarded[dz, dx].arrive()
        rows = aligned(source, BLOCK)
        product = dot_nn(r.row[source].reshape(BLOCK, 1024), r.head_weights[...])
        r.raw[rows, :] = product[:, :384]
        r.values[rows, :] = product[:, 384:].astype(BF16)
        for part in range(3):
            gain = r.query_gain[...] if part < 2 else r.key_gain[...]
            normed, inverse = normalize(product[:, part * HD : (part + 1) * HD], gain)
            r.inverses[rows, part : part + 1] = inverse
            turned = normed * r.cosines[rows, :] + pltpu.roll(normed, 64, 1) * r.sines[rows, :]
            if part < 2:
                r.queries[rows, part * HD : (part + 1) * HD] = turned.astype(BF16)
            else:
                r.keys[rows, :] = turned.astype(BF16)

    for load in loads:
        load.wait()
    forward_blocks(0)
    forward_blocks(1)
    project(0)
    forward_blocks(3)
    project(1)
    forward_blocks(2)
    project(3)
    for landing in document_landings:
        landing.arrive()
    document_landings_own.wait()
    lane = lax.broadcasted_iota(jnp.int32, (1, 128), 1)
    pieces = []
    for block in range(8):
        even = r.row_documents[block // 2, block % 2, 0, 0:1, :]
        odd = r.row_documents[block // 2, block % 2, 1, 0:1, :]
        piece = jnp.where(lane < 64, even, odd)
        pieces.append(piece)
        r.document_column[block * 128 : (block + 1) * 128, :] = jnp.broadcast_to(piece, (128, 128)).T
    document_row = jnp.concatenate(pieces, axis=1)
    project(2)

    def visible_in(block):
        count = (block + 1) * BLOCK
        rows = slice(block * BLOCK, count)
        same = r.document_column[rows, 0:1] == document_row[:, :count]
        row_at = block * BLOCK + lax.broadcasted_iota(jnp.int32, (BLOCK, count), 0)
        column_at = lax.broadcasted_iota(jnp.int32, (BLOCK, count), 1)
        return same & (row_at >= column_at)

    attn_landings = []
    for h in range(2):
        columns = slice(h * HD, (h + 1) * HD)
        for block in range(4):
            rows = slice(block * BLOCK, (block + 1) * BLOCK)
            count = (block + 1) * BLOCK
            scores = dot_nt(r.queries[rows, columns], r.keys[:count, :])
            scores = jnp.where(visible_in(block), scores * (SCALE * LOG2E), MASKED)
            top = jnp.max(scores, axis=-1, keepdims=True)
            soft = jnp.exp2(scores - top)
            total = jnp.sum(soft, axis=-1, keepdims=True)
            mixed = dot_nn(soft.astype(BF16), r.values[:count, :]) / total
            r.attended[rows, columns] = mixed
            r.attn_heads[block, :, :, :, columns] = mixed.astype(BF16).reshape(2, 2, 64, HD)
            r.log_total[rows, h : h + 1] = top + jnp.log2(total)
        here = pl.ds(pl.multiple_of(head * 256 + h * HD, HD), HD)
        for t in zc:
            attn_landings.append(
                net.send(r.attn_heads.at[t[2], :, t[4], :, pl.ds(h * HD, HD)], r.attn_tokens.at[:, :, here], t)
            )
        attn_landings.append(
            net.keep(r.attn_heads.at[z, :, c, :, pl.ds(h * HD, HD)], r.attn_tokens.at[:, :, here])
        )
    for landing in attn_landings:
        landing.arrive() if isinstance(landing, Landing) else landing.wait()

    def chain(axis, src, slot_of):
        steps = []
        for step in (1, 3, 2):
            shift = {"d" + axis: step}
            back = {"d" + axis: -step}
            source = shifted(at, **back)
            steps.append((net.send(src, slot_of(at), shifted(at, **shift)), slot_of(source)))
        last = [net.send(src, slot_of(at), sibling)]
        own = net.keep(src, slot_of(at))
        return (steps, last, own)

    def chain_forward(state):
        steps, last, own = state
        for landing, slot in steps:
            landing.arrive()
            last.append(net.send(slot, slot, sibling))

    def chain_arrive(state):
        steps, last, own = state
        for landing in last:
            landing.arrive()
        own.wait()

    load_wo.wait()
    branch = dot_nt(r.wo[...], r.attn_tokens[...].reshape(128, 2048)).T
    r.branch[...] = branch
    branch_normed, branch_inverse = normalize(branch, r.attention_gain[...])
    residual = r.row[z, :, c].reshape(128, 1024).astype(F32) + branch_normed
    r.residual[...] = residual
    r.residual_low[...] = residual.astype(BF16)
    residual_chain = chain(
        "y", r.residual_low, lambda who: r.residual_all.at[aligned(who[1] * 2 + who[4], 128), :]
    )
    for load in load_wgu:
        load.wait()
    for tile in range(6):
        columns = slice(tile * 512, (tile + 1) * 512)
        up_columns = slice(3072 + tile * 512, 3072 + (tile + 1) * 512)
        gate = dot_nn(r.residual_low[...], r.wgu[:, columns])
        up = dot_nn(r.residual_low[...], r.wgu[:, up_columns])
        sigmoid_gate = lax.logistic(gate)
        silu = gate * sigmoid_gate
        r.activated[:, columns] = (silu * up).astype(BF16)
        r.up_factor[:, columns] = silu
        r.gate_factor[:, columns] = up * sigmoid_gate * (1.0 + gate * (1.0 - sigmoid_gate))

    x_slot = aligned(x * 2 + c, 128)
    y_slot = aligned(y * 2 + c, 128)
    activated_landings = [
        net.send(
            r.activated.at[:, aligned((t[0] * 2 + t[3]) * 2 + t[4], 384)], r.activated_all.at[x_slot, :], t
        )
        for t in xc
    ]
    activated_own = net.keep(r.activated.at[:, aligned(x * 2 + c, 384)], r.activated_all.at[x_slot, :])
    load_wd.wait()
    down = dot_nt(r.wd[...], r.activated[...]).T
    upstream_landing.arrive()
    upstream_own.wait()
    down_normed, down_inverse = normalize(down, r.feedforward_gain[...])
    r.layer_output[...] = (r.residual[...] + down_normed).reshape(2, 64, 1024)
    upstream = r.upstream[...].reshape(128, 1024).astype(F32)
    down_grad, feedforward_gain_grad = norm_back(upstream, down, down_inverse, r.feedforward_gain[...])
    r.down_low[...] = down_grad.astype(BF16)
    down_chain = chain(
        "x", r.down_low, lambda who: r.down_all.at[aligned((who[0] * 2 + who[3]) * 2 + who[4], 128), :]
    )
    for tile in range(6):
        columns = slice(tile * 512, (tile + 1) * 512)
        up_columns = slice(3072 + tile * 512, 3072 + (tile + 1) * 512)
        act_grad = dot_nn(r.down_low[...], r.wd[:, columns])
        r.gate_up_low[:, columns] = (act_grad * r.gate_factor[:, columns]).astype(BF16)
        r.gate_up_low[:, up_columns] = (act_grad * r.up_factor[:, columns]).astype(BF16)
    chain_forward(residual_chain)
    gate_up_landings = []
    for part in range(2):
        for t in yc:
            gate_up_landings.append(
                net.send(
                    r.gate_up_low.at[:, aligned(part * 8 + t[1] * 2 + t[4], 384)],
                    r.gate_up_all.at[y_slot, pl.ds(part * 384, 384)],
                    t,
                )
            )
    gate_up_own = [
        net.keep(
            r.gate_up_low.at[:, aligned(part * 8 + y * 2 + c, 384)],
            r.gate_up_all.at[y_slot, pl.ds(part * 384, 384)],
        )
        for part in range(2)
    ]
    residual_grad = upstream + dot_nt(r.wgu[...], r.gate_up_low[...]).T
    r.residual_grad[...] = residual_grad
    branch_grad, attention_gain_grad = norm_back(
        residual_grad, r.branch[...], branch_inverse, r.attention_gain[...]
    )
    for i in range(8):
        r.gains_own[i : i + 1, :] = attention_gain_grad[:, i * 128 : (i + 1) * 128]
        r.gains_own[8 + i : 9 + i, :] = feedforward_gain_grad[:, i * 128 : (i + 1) * 128]
    branch_low = branch_grad.astype(BF16)
    r.branch_low[...] = branch_low.reshape(2, 64, 1024)
    r.attn_grad[...] = dot_nn(branch_low, r.wo[...]).astype(BF16).reshape(2, 64, 2048)
    attn_grad_landings = [
        net.send(r.attn_grad.at[:, :, aligned(t[2] * 2 + t[4], 256)], r.attn_grad_row.at[z, :, c], t)
        for t in zc
    ]
    attn_grad_own = net.keep(r.attn_grad.at[:, :, aligned(head, 256)], r.attn_grad_row.at[z, :, c])
    branch_chain = chain("z", r.branch_low, lambda who: r.branch_row.at[who[2], :, who[4]])
    out_landing = net.send(r.layer_output.at[1 - xl], r.out.at[xl], partner)
    out_own = net.keep(r.layer_output.at[xl], r.out.at[xl])
    head_loads = []
    for i in range(8):
        for ref, start, width in (
            (r.query_weight, 0, 256),
            (r.key_weight, 256, 128),
            (r.value_weight, 384, 128),
        ):
            head_loads.append(
                net.keep(ref.at[:, pl.ds(i * width, width)], r.wgu.at[:, pl.ds(i * 512 + start, width)])
            )
    chain_forward(down_chain)

    r.key_sum[...] = jnp.zeros_like(r.key_sum)
    r.value_sum[...] = jnp.zeros_like(r.value_sum)
    for landing in attn_grad_landings:
        landing.arrive()
    attn_grad_own.wait()

    def rope_norm_back(grad, part, rows, gain):
        turned = grad * r.cosines[rows, :] - pltpu.roll(grad, 64, 1) * r.sines[rows, :]
        vector = r.raw[rows, part * HD : (part + 1) * HD]
        result, gain_part = norm_back(turned, vector, r.inverses[rows, part : part + 1], gain)
        return (result.astype(BF16).reshape(2, 2, 64, HD), gain_part)

    query_total = jnp.zeros((1, HD), F32)
    for block in range(4):
        rows = slice(block * BLOCK, (block + 1) * BLOCK)
        count = (block + 1) * BLOCK
        visible = visible_in(block)
        for h in range(2):
            columns = slice(h * HD, (h + 1) * HD)
            query = r.queries[rows, columns]
            grad = r.attn_grad_row[block, :, :, :, columns].reshape(BLOCK, HD)
            delta = jnp.sum(grad.astype(F32) * r.attended[rows, columns], axis=-1, keepdims=True)
            scores = dot_nt(query, r.keys[:count, :]) * (SCALE * LOG2E)
            soft = jnp.exp2(jnp.where(visible, scores - r.log_total[rows, h : h + 1], MASKED))
            r.value_sum[:count, :] += dot_tn(soft.astype(BF16), grad)
            soft_grad = dot_nt(grad, r.values[:count, :])
            score_low = (soft * (soft_grad - delta)).astype(BF16)
            query_grad = dot_nn(score_low, r.keys[:count, :]) * SCALE
            r.key_sum[:count, :] += dot_tn(score_low, query)
            low, gain_part = rope_norm_back(query_grad, h, rows, r.query_gain[...])
            r.lows[block, :, :, :, columns] = low
            query_total = query_total + gain_part
    key_total = jnp.zeros((1, HD), F32)
    for block in range(4):
        rows = slice(block * BLOCK, (block + 1) * BLOCK)
        low, gain_part = rope_norm_back(r.key_sum[rows, :] * SCALE, 2, rows, r.key_gain[...])
        r.lows[block, :, :, :, 256:384] = low
        r.lows[block, :, :, :, 384:] = r.value_sum[rows, :].astype(BF16).reshape(2, 2, 64, HD)
        key_total = key_total + gain_part
    r.gains_own[16:17, :] = query_total
    r.gains_own[17:18, :] = key_total
    r.gains_own[18:24, :] = jnp.zeros((6, 128), F32)
    low_landings = [
        net.send(r.lows.at[t[2], :, t[4]], r.low_tokens.at[:, :, aligned(head, 512)], t) for t in zc
    ]
    low_own = net.keep(r.lows.at[z, :, c], r.low_tokens.at[:, :, aligned(head, 512)])
    gains_y = [net.send(r.gains_own, r.gains_y.at[i], ys[i]) for i in range(3)]

    chain_forward(branch_chain)
    row = r.row[...].reshape(1024, 1024)
    low_columns = dot_tn(row, r.lows[...].reshape(1024, 512)).astype(BF16)
    r.own_a[..., 0:384] = low_columns[:, :384].reshape(4, 2, 2, 4, 16, 384)
    r.own_a[..., 640:768] = low_columns[:, 384:].reshape(4, 2, 2, 4, 16, 128)
    chain_arrive(residual_chain)
    for landing in gate_up_landings:
        landing.arrive()
    for copy in gate_up_own:
        copy.wait()
    load_b = [
        net.keep(r.residual_all, r.wo.at[:, pl.ds(0, 1024)]),
        net.keep(r.gate_up_all, r.wd.at[:, pl.ds(0, 768)]),
    ]
    chain_arrive(branch_chain)
    output_columns = dot_tn(
        r.branch_row[...].reshape(1024, 1024), r.attn_heads[...].reshape(1024, 256)
    ).astype(BF16)
    r.own_a[..., 384:640] = output_columns.reshape(4, 2, 2, 4, 16, 256)
    first_a = [net.send(r.own_a.at[:, :, :, ys[i][1]], r.all_a.at[i], ys[i]) for i in range(3)]
    for load in load_b:
        load.wait()
    r.own_b[...] = dot_tn(r.wo[:, :1024], r.wd[:, :768]).astype(BF16).reshape(4, 2, 2, 64, 768)
    first_b = [
        net.send(r.own_b.at[:, t[3], :, :, aligned(t[0], 384)], r.all_b.at[i], t) for i, t in enumerate(xs)
    ]
    chain_arrive(down_chain)
    for landing in activated_landings:
        landing.arrive()
    activated_own.wait()
    load_c = [
        net.keep(r.down_all, r.wo.at[:, pl.ds(1024, 1024)]),
        net.keep(r.activated_all, r.wd.at[:, pl.ds(768, 384)]),
    ]
    for load in load_c:
        load.wait()
    r.own_c[...] = dot_tn(r.wo[:, 1024:], r.wd[:, 768:1152]).astype(BF16).reshape(4, 2, 2, 4, 16, 384)
    first_c = [net.send(r.own_c.at[t[2]], r.all_c.at[i], t) for i, t in enumerate(zs)]

    for load in head_loads:
        load.wait()
    for landing in low_landings:
        landing.arrive()
    low_own.wait()
    input_grad = r.residual_grad[...] + dot_nt(r.wgu[:, :4096], r.low_tokens[...].reshape(128, 4096)).T
    r.input_grad[...] = input_grad.reshape(2, 64, 1024)
    grad_landing = net.send(r.input_grad.at[1 - xl], r.grad.at[xl], partner)
    grad_own = net.keep(r.input_grad.at[xl], r.grad.at[xl])

    def total(own, others, landings):
        for landing in landings:
            landing.arrive()
        result = own.astype(F32)
        for i in range(len(landings)):
            result = result + others[i].astype(F32)
        return result

    r.gains_next[...] = total(r.gains_own[...], r.gains_y, gains_y)
    gains_x = [net.send(r.gains_next, r.gains_x.at[i], xs[i]) for i in range(3)]
    r.next_c[...] = total(r.own_c[z], r.all_c, first_c).astype(BF16)
    then_c = [net.send(r.next_c.at[:, :, t[1]], r.then_c.at[i], t) for i, t in enumerate(ys)]
    mine = aligned(xh, 384)
    r.next_b[...] = total(r.own_b[:, xl, :, :, mine], r.all_b, first_b).astype(BF16)
    then_b = [net.send(r.next_b.at[t[2]], r.then_b.at[i], t) for i, t in enumerate(zs)]
    r.next_a[...] = total(r.own_a[:, :, :, y], r.all_a, first_a).astype(BF16)
    then_a = [
        net.send(r.next_a.at[:, t[3], :, :, aligned(t[0], 384)], r.then_a.at[i], t) for i, t in enumerate(xs)
    ]

    r.done_c[...] = total(r.next_c[:, :, y], r.then_c, then_c).astype(BF16)
    quarter = aligned(xl * 2 + c, 384)
    pairs = [partner, shifted(at, flip_xl=1, dc=1), sibling]
    got_c = [net.send(r.done_c.at[t[3], t[4]], r.got_c.at[:, quarter], t) for t in pairs]
    got_c_own = net.keep(r.done_c.at[xl, c], r.got_c.at[:, quarter])
    r.done_b[...] = total(r.next_b[z], r.then_b, then_b).astype(BF16)
    got_b = net.send(r.done_b.at[1 - c], r.got_b.at[:, aligned(c, 384)], sibling)
    got_b_own = net.keep(r.done_b.at[c], r.got_b.at[:, aligned(c, 384)])
    r.gains_last[...] = total(r.gains_next[...], r.gains_x, gains_x)
    gains_zc = [net.send(r.gains_last, r.gains_zc.at[i], t) for i, t in enumerate(zc)]
    r.done_a[...] = total(r.next_a[:, xl, :, :, mine], r.then_a, then_a).astype(BF16)
    got_a = []
    for t in zc:
        got_a.append(net.send(r.done_a.at[t[2], t[4], :, pl.ds(0, 256)], r.got_wide.at[:, aligned(head, 256)], t))
        got_a.append(net.send(r.done_a.at[t[2], t[4], :, pl.ds(256, 128)], r.got_narrow.at[:, aligned(head, 128)], t))
    got_a_own = [
        net.keep(r.done_a.at[z, c, :, pl.ds(0, 256)], r.got_wide.at[:, aligned(head, 256)]),
        net.keep(r.done_a.at[z, c, :, pl.ds(256, 128)], r.got_narrow.at[:, aligned(head, 128)]),
    ]

    ending = []

    def spread(src, slot):
        for t in replicas:
            ending.append(net.send(src, slot, t))
        ending.append(net.keep(src, slot))

    got_b.arrive()
    got_b_own.wait()
    spread(r.got_b, r.gate_up_grad.at[xh, :, aligned(y, 768)])
    for landing in got_c:
        landing.arrive()
    got_c_own.wait()
    spread(r.got_c, r.down_grad.at[aligned(y, 16), aligned(xh, 1536)])
    for landing in got_a:
        landing.arrive()
    for copy in got_a_own:
        copy.wait()
    spread(r.got_wide, r.wide.at[xh, aligned(y, 16), :])
    spread(r.got_narrow, r.narrow.at[xh, aligned(y, 16), :])
    r.gains_final[...] = total(r.gains_last[...], r.gains_zc, gains_zc)
    gains_out = net.keep(r.gains_final, r.gains)
    for item in ending:
        if not isinstance(item, Landing):
            item.wait()
    for copy in (out_own, grad_own, gains_out):
        copy.wait()
    net.drain()


def layer(*arrays):
    return pl.pallas_call(
        layer_kernel,
        out_shape=[shape(dims, dtype) for _, dims, dtype in OUTPUTS],
        in_specs=[
            pl.BlockSpec(memory_space=pltpu.VMEM if name in IN_VMEM else pl.ANY) for name in INPUTS
        ],
        out_specs=[pl.BlockSpec(memory_space=pl.ANY)] * len(OUTPUTS),
        scratch_shapes=[pltpu.VMEM(dims, dtype) for _, dims, dtype in SCRATCH]
        + [
            pltpu.SemaphoreType.DMA((SENDS,)),
            pltpu.SemaphoreType.DMA((SENDS,)),
            pltpu.SemaphoreType.DMA((KEEPS,)),
        ],
        compiler_params=pltpu.CompilerParams(
            collective_id=0, has_side_effects=True, vmem_limit_bytes=VMEM_LIMIT
        ),
        name="layer",
    )(*arrays)


VMEM_LIMIT = 63 * 2**20


def per_device(
    hidden_in,
    query_weight,
    key_weight,
    value_weight,
    output_weight,
    gate_weight,
    up_weight,
    down_weight,
    query_gain,
    key_gain,
    attention_gain,
    feedforward_gain,
    document_ids,
    cotangent,
):
    documents = document_ids.astype(F32)
    documents = jnp.concatenate([documents, documents], axis=1)
    documents = jnp.broadcast_to(documents[:, None, :], (2, 8, 128))
    out, grad, wide, narrow, gate_up_grad, down_grad, gains = layer(
        hidden_in, cotangent, documents,
        query_weight, key_weight, value_weight, output_weight, gate_weight, up_weight, down_weight,
        *rope_tables(),
        query_gain[None, :], key_gain[None, :], attention_gain[None, :], feedforward_gain[None, :],
    )[:7]
    return (
        out,
        grad,
        wide[0].astype(F32),
        narrow[0].astype(F32),
        narrow[1].astype(F32),
        wide[1].astype(F32),
        gate_up_grad[0].astype(F32),
        gate_up_grad[1].astype(F32),
        down_grad.astype(F32),
        gains[16],
        gains[17],
        gains[:8].reshape(1024),
        gains[8:16].reshape(1024),
    )


def solution(mesh):
    tokens = P("rows", "seq", None)
    split = P("seq", None)
    return jax.shard_map(
        per_device,
        mesh=mesh,
        in_specs=(tokens,) + (P(),) * 11 + (P("rows", "seq"), tokens),
        out_specs=(tokens, tokens) + (split,) * 7 + (P(),) * 4,
        check_vma=False,
    )
```

profile of v0, /device:TPU:1, one launch (start us, length us, event | category | flops | bytes accessed | tf_op | source)
XLA Modules:
  0.0 153.2 jit_solution(403404240145951921)
XLA Ops:
  0.6 0.7 convert_element_type.42
  1.3 0.1 pad_maximum_fusion
  1.4 0.6 broadcast_in_dim.18.refs_2_
  2.0 138.7 %layer.1 = (f32[2,64,1024]{2,1,0:T(8,128)}, f32[2,64,1024]{2,1,0:T(8,128)}, bf16[2,64,2048]{2,1,0:T(8,128)(2,1)}, bf16[2,64,1024]{2,1,0:T(8,128)(2,1)}, bf16[2,6...) custom-call(bf16[2,64,1024]{2,1,0:T(8,128)(2,1)} %refs_0_.1, ...), custom_call_target="tpu_custom_call" | custom-call | tf_op jit(solution)/shard_map/layer/pallas_call | solution.py:671
  140.8 0.0 copy-start.1
  140.8 0.0 copy-start
  140.8 1.3 slice_bitcast_fusion.2
  142.1 1.3 slice_bitcast_fusion
  143.4 1.8 %bitcast_convert_fusion.4 = (f32[64,1024]{1,0:T(8,128)}, f32[64,1024]{1,0:T(8,128)}) fusion(bf16[2,64,1024]{2,1,0:T(8,128)(2,1)} %get-tuple-element.23), kind=kLoop, calls=%fused_computation.4 | loop fusion | flops 131072 | bytes 786432 | tf_op jit(solution)/shard_map/convert_element_type | solution.py:724
  145.2 1.9 %convert_element_type.55 = f32[64,3072]{1,0:T(8,128)} convert(bf16[64,3072]{1,0:T(8,128)(2,1)} %get-tuple-element.25) | non-fusion elementwise | flops 196608 | bytes 1179648 | tf_op jit(solution)/shard_map/convert_element_type | solution.py:728
  147.1 2.1 %bitcast_convert_fusion.2 = (f32[64,2048]{1,0:T(8,128)}, f32[64,2048]{1,0:T(8,128)}) fusion(bf16[2,64,2048]{2,1,0:T(8,128)(2,1)} %get-tuple-element.22), kind=kLoop, calls=%fused_computation.2 | loop fusion | flops 262144 | bytes 1572864 | tf_op jit(solution)/shard_map/convert_element_type | solution.py:725
  149.2 2.4 %bitcast_convert_fusion = (f32[64,3072]{1,0:T(8,128)}, f32[64,3072]{1,0:T(8,128)}) fusion(bf16[2,64,3072]{2,1,0:T(8,128)(2,1)} %get-tuple-element.24), kind=kLoop, calls=%fused_computation | loop fusion | flops 393216 | bytes 2359296 | tf_op jit(solution)/shard_map/convert_element_type | solution.py:727
  151.6 0.0 copy-done.1
  151.6 0.8 copy.31
  152.4 0.0 copy-done
  152.4 0.8 copy.32
Async XLA Ops:
  140.8 10.8 %copy-start.1 = (f32[2,64,1024]{2,1,0:T(8,128)S(1)}, f32[2,64,1024]{2,1,0:T(8,128)}, u32[]{:S(2)}) copy-start(f32[2,64,1024]{2,1,0:T(8,128)} %get-tuple-element.50) | copy-start | bytes 1572868
  140.8 11.6 %copy-start = (f32[2,64,1024]{2,1,0:T(8,128)S(1)}, f32[2,64,1024]{2,1,0:T(8,128)}, u32[]{:S(2)}) copy-start(f32[2,64,1024]{2,1,0:T(8,128)} %get-tuple-element.51) | copy-start | bytes 1572868
where the time goes:
time: 156 us; the launch traced here: 153 us
  Pallas kernels  139 us (89%)
  other arithmetic  9 us (6%)
  local copies, waits for them, and re-layouts  4.77 us (3%)
    pallas_call x1, Pallas kernels, layer(): pl.pallas_call(layer_kernel, out_shape=[shape(dims, dtype) for _, dims, d...  139 us

commit v1 on v0

v1 whole, which is shorter than its diff:
```python
import functools

import jax
import jax.numpy as jnp
import numpy as np
from jax import lax
from jax.experimental import pallas as pl
from jax.experimental.pallas import tpu as pltpu
from jax.sharding import PartitionSpec as P

HD = 128
EPSILON = 1e-06
ROPE_BASE = 1000000.0
MASKED = -1e30
LOG2E = 1.4426950408889634
SCALE = HD ** (-0.5)
MESH = pl.DeviceIdType.MESH
F32 = jnp.float32
BF16 = jnp.bfloat16

YS = 4
ZS = 4
XS = 4


def place():
    rows, seq = lax.axis_index("rows"), lax.axis_index("seq")
    return (rows // YS, rows % YS, seq // 4, (seq // 2) % 2, seq % 2)


def device(xh, y, z, xl, c):
    return (xh * YS + y, z * 4 + xl * 2 + c)


def shifted(at, dx=0, dy=0, dz=0, dc=0, flip_xl=0, flip_xh=0):
    xh, y, z, xl, c = at
    if dx:
        x = (xh * 2 + xl + dx) % XS
        xh, xl = x // 2, x % 2
    if flip_xl:
        xl = 1 - xl
    if flip_xh:
        xh = 1 - xh
    if dc:
        c = 1 - c
    return (xh, (y + dy) % YS, (z + dz) % ZS, xl, c)


class Group:
    def __init__(self, net, index):
        self.net, self.index = net, index
        self.units, self.here = 0, False

    def add(self, src, dst, target, start=True):
        copy = self.net.remote(src, dst, target, self.index)
        if start:
            copy.start()
        self.units += units_of(dst)
        return self

    def wait(self):
        if not self.here:
            self.net.sized(self.units, self.net.recv_sems.at[self.index]).wait()
            self.here = True

    def drain(self):
        self.wait()
        self.net.sized(self.units, self.net.send_sems.at[self.index]).wait()


class LocalGroup:
    def __init__(self, net, index):
        self.net, self.index = net, index
        self.units, self.here, self.only = 0, False, None

    def add(self, src, dst):
        copy = pltpu.make_async_copy(src, dst, self.net.local_sems.at[self.index])
        copy.start()
        self.only = None if self.units else copy
        self.units += units_of(dst)
        return self

    def wait(self):
        if not self.here:
            if self.only is None:
                self.net.sized(self.units, self.net.local_sems.at[self.index]).wait()
            else:
                self.only.wait()
            self.here = True


def units_of(ref):
    return int(np.prod(ref.shape)) * (1 if ref.dtype == BF16 else 2)


class Net:
    def __init__(self, send_sems, recv_sems, local_sems, measures):
        self.send_sems, self.recv_sems, self.local_sems = send_sems, recv_sems, local_sems
        self.measures = measures
        self.groups, self.locals, self.next_send, self.next_keep = [], [], 0, 0

    def sized(self, units, sem):
        for ref in self.measures:
            columns = ref.shape[-1]
            while columns >= 128:
                rows = units // columns
                if rows * columns == units and rows % 16 == 0 and rows <= ref.shape[0] and columns % 128 == 0:
                    view = ref.at[pl.ds(0, rows), pl.ds(0, columns)]
                    return pltpu.make_async_copy(view, view, sem)
                columns -= 128
        raise ValueError(units)

    def barrier(self, targets):
        barrier = pltpu.get_barrier_semaphore()
        for target in targets:
            pl.semaphore_signal(barrier, inc=1, device_id=device(*target), device_id_type=MESH)
        pl.semaphore_wait(barrier, len(targets))

    def remote(self, src, dst, target, i):
        return pltpu.make_async_remote_copy(
            src_ref=src,
            dst_ref=dst,
            send_sem=self.send_sems.at[i],
            recv_sem=self.recv_sems.at[i],
            device_id=device(*target),
            device_id_type=MESH,
        )

    def group(self):
        self.groups.append(Group(self, self.next_send))
        self.next_send += 1
        return self.groups[-1]

    def local_group(self):
        self.locals.append(LocalGroup(self, self.next_keep))
        self.next_keep += 1
        return self.locals[-1]

    def send(self, src, dst, target):
        return self.group().add(src, dst, target)

    def together(self, items):
        result = self.group()
        for src, dst, target in items:
            result.add(src, dst, target)
        return result

    def keep(self, src, dst):
        return self.local_group().add(src, dst)

    def drain(self):
        for group in self.locals:
            group.wait()
        for group in self.groups:
            group.drain()


def shape(dims, dtype=BF16):
    return jax.ShapeDtypeStruct(dims, dtype)


ZC = [(dz, dc) for dz in range(ZS) for dc in range(2) if (dz, dc) != (0, 0)]
ORDER = (0, 1, 3, 2)
BLOCK = 256
SENDS = 87
KEEPS = 39


def rope_tables():
    half = HD // 2
    frequency = ROPE_BASE ** (-(np.arange(half, dtype=np.float64) * 2.0 / HD))
    angles = np.arange(1024, dtype=np.float64)[:, None] * frequency[None, :]
    cosines = np.concatenate([np.cos(angles)] * 2, axis=1)
    sines = np.concatenate([-np.sin(angles), np.sin(angles)], axis=1)
    return (cosines.astype(np.float32), sines.astype(np.float32))


def dot_nn(left, right):
    return jnp.dot(left, right, preferred_element_type=F32)


def dot_nt(left, right):
    return lax.dot_general(left, right, (((1,), (1,)), ((), ())), preferred_element_type=F32)


def dot_tn(left, right):
    return lax.dot_general(left, right, (((0,), (0,)), ((), ())), preferred_element_type=F32)


def normalize(vector, scales):
    inverse = lax.rsqrt(jnp.mean(vector * vector, axis=-1, keepdims=True) + EPSILON)
    return (vector * inverse * scales, inverse)


def norm_back(gradient, vector, inverse, scales):
    normed = vector * inverse
    scales_grad = jnp.sum(gradient * normed, axis=0, keepdims=True)
    scaled = gradient * scales
    vector_grad = inverse * (scaled - normed * jnp.mean(scaled * normed, axis=-1, keepdims=True))
    return (vector_grad, scales_grad)


def aligned(index, width):
    return pl.ds(pl.multiple_of(index * width, width), width)


class Refs:
    pass


INPUTS = dict(
    hidden=0,
    cotangent=0,
    query_weight=0,
    key_weight=0,
    value_weight=0,
    output_weight=0,
    gate_weight=0,
    up_weight=0,
    down_weight=0,
    document_ids_in=((2, 64), jnp.int32),
    cosines_in=((1024, 128), F32),
    sines_in=((1024, 128), F32),
    query_gain_in=((1, 128), F32),
    key_gain_in=((1, 128), F32),
    attention_gain_in=((1, 1024), F32),
    feedforward_gain_in=((1, 1024), F32),
)
SMALL = {name[:-3]: item for name, item in INPUTS.items() if item}
OUTPUTS = dict(
    out_own=((64, 1024), F32),
    grad_own=((64, 1024), F32),
    out_got=((64, 1024), BF16),
    grad_got=((64, 1024), BF16),
    query_weight_grad=((64, 2048), BF16),
    key_value_grad=((2, 64, 1024), BF16),
    output_weight_grad=((64, 2048), BF16),
    gate_grad=((64, 3072), BF16),
    up_grad=((64, 3072), BF16),
    down_grad=((64, 3072), BF16),
    gains=((24, 128), F32),
    residual_y=((1024, 1024), BF16),
    gate_all=((1024, 384), BF16),
    up_all=((1024, 384), BF16),
    down_all=((1024, 1024), BF16),
    activated_all=((1024, 384), BF16),
)
SCRATCH = dict(
    head_weights=((1024, 512), BF16),
    wo=((1024, 2048), BF16),
    wgu=((1024, 6144), BF16),
    wd=((1024, 3072), BF16),
    row=((4, 2, 2, 64, 1024), BF16),
    upstream=((2, 64, 1024), BF16),
    documents=((2, 16, 128), F32),
    row_documents=((16, 16, 128), F32),
    document_column=((1024, 128), F32),
    raw=((1024, 384), F32),
    inverses=((1024, 3), F32),
    queries=((1024, 256), BF16),
    keys=((1024, 128), BF16),
    values=((1024, 128), BF16),
    attended=((1024, 256), F32),
    attn_heads=((4, 2, 2, 64, 256), BF16),
    log_total=((2, 1024, 1), F32),
    attn_tokens=((2, 64, 2048), BF16),
    branch=((128, 1024), F32),
    down=((128, 1024), F32),
    residual=((128, 1024), F32),
    residual_low=((128, 1024), BF16),
    gate_factor=((128, 3072), F32),
    up_factor=((128, 3072), F32),
    activated=((128, 3072), BF16),
    layer_output=((2, 64, 1024), F32),
    down_low=((128, 1024), BF16),
    gate_up_low=((128, 6144), BF16),
    residual_grad=((128, 1024), F32),
    branch_low=((2, 64, 1024), BF16),
    attn_grad=((2, 64, 2048), BF16),
    attn_grad_row=((4, 2, 2, 64, 256), BF16),
    branch_row=((4, 2, 2, 64, 1024), BF16),
    lows=((4, 2, 2, 64, 512), BF16),
    key_sum=((1024, 128), F32),
    value_sum=((1024, 128), F32),
    low_tokens=((2, 64, 4096), BF16),
    input_grad=((2, 64, 1024), F32),
    out_low=((2, 64, 1024), BF16),
    grad_low=((2, 64, 1024), BF16),
    own_gate=((4, 2, 2, 2, 32, 384), BF16),
    all_gate=((3, 2, 2, 2, 32, 384), BF16),
    next_gate=((2, 2, 2, 32, 384), BF16),
    then_gate=((3, 2, 32, 384), BF16),
    done_gate=((2, 32, 384), BF16),
    got_gate=((32, 768), BF16),
    own_query=((4, 2, 2, 4, 16, 256), BF16),
    all_query=((3, 4, 2, 2, 16, 256), BF16),
    next_query=((4, 2, 2, 16, 256), BF16),
    then_query=((3, 4, 2, 16, 256), BF16),
    done_query=((4, 2, 16, 256), BF16),
    got_query=((16, 2048), BF16),
    own_kv=((4, 2, 2, 4, 16, 256), BF16),
    all_kv=((3, 4, 2, 4, 16, 128), BF16),
    next_kv=((4, 2, 4, 16, 128), BF16),
    then_kv=((3, 4, 2, 16, 128), BF16),
    done_kv=((4, 2, 16, 128), BF16),
    got_kv=((16, 1024), BF16),
    own_output=((4, 2, 2, 4, 16, 256), BF16),
    all_output=((3, 4, 2, 2, 16, 256), BF16),
    next_output=((4, 2, 2, 16, 256), BF16),
    then_output=((3, 4, 2, 16, 256), BF16),
    done_output=((4, 2, 16, 256), BF16),
    got_output=((16, 2048), BF16),
    own_up=((4, 2, 2, 2, 32, 384), BF16),
    all_up=((3, 4, 2, 32, 384), BF16),
    next_up=((4, 2, 32, 384), BF16),
    then_up=((3, 2, 32, 384), BF16),
    done_up=((2, 32, 384), BF16),
    got_up=((32, 768), BF16),
    own_down=((4, 2, 2, 4, 16, 384), BF16),
    all_down=((3, 4, 2, 2, 16, 384), BF16),
    next_down=((4, 2, 2, 16, 384), BF16),
    then_down=((3, 2, 2, 16, 384), BF16),
    done_down=((2, 2, 16, 384), BF16),
    got_down=((16, 1536), BF16),
    gains_own=((24, 128), F32),
    gains_next=((24, 128), F32),
    gains_last=((24, 128), F32),
    gains_final=((24, 128), F32),
    gains_y=((3, 24, 128), F32),
    gains_x=((3, 24, 128), F32),
    gains_zc=((7, 24, 128), F32),
)


def layer_kernel(*refs):
    names = [*INPUTS, *OUTPUTS, *SCRATCH, *SMALL]
    r = Refs()
    for name, ref in zip(names, refs):
        setattr(r, name, ref)
    net = Net(*refs[len(names) :], (r.wd, r.wgu))
    at = place()
    xh, y, z, xl, c = at
    x = xh * 2 + xl
    head = z * 2 + c
    sibling = shifted(at, dc=1)
    partner = shifted(at, flip_xl=1)
    seq_others = [
        shifted(at, dz=dz, dc=dc, flip_xl=dx)
        for dz in range(ZS)
        for dx in range(2)
        for dc in range(2)
        if (dz, dx, dc) != (0, 0, 0)
    ]
    zc = [shifted(at, dz=dz, dc=dc) for dz, dc in ZC]
    yc = [shifted(at, dy=dy, dc=dc) for dy, dc in ZC]
    xc = [shifted(at, dx=dx, dc=dc) for dx, dc in ZC]
    ys = [shifted(at, dy=step) for step in range(1, 4)]
    xs = [shifted(at, dx=step) for step in range(1, 4)]
    zs = [shifted(at, dz=step) for step in range(1, 4)]
    replicas = [
        shifted(at, dy=dy, flip_xh=dx) for dy in range(YS) for dx in range(2) if (dy, dx) != (0, 0)
    ]

    barrier_targets = list(seq_others) + yc[1:] + xc[1:] + replicas
    documents_load = net.keep(r.document_ids_in, r.document_ids)
    net.barrier(barrier_targets)
    up_z, down_z = shifted(at, dz=1), shifted(at, dz=-1)
    arrived = {}
    arrived[0, 1] = net.send(r.hidden.at[1 - xl], r.row.at[z, xl, c], partner)
    for dz, target in ((1, up_z), (3, down_z)):
        arrived[dz, 0] = net.send(r.hidden.at[xl], r.row.at[z, xl, c], target)
    own_block = net.keep(r.hidden.at[xl], r.row.at[z, xl, c])
    documents_load.wait()
    own_documents = r.document_ids[...].astype(F32)
    own_documents = jnp.concatenate([own_documents, own_documents], axis=1)
    for i in range(2):
        r.documents[i] = jnp.broadcast_to(own_documents[i : i + 1, :], (16, 128))
    document_slot = r.row_documents.at[z * 4 + xl * 2 + c]
    document_landings = net.together([(r.documents.at[t[3]], document_slot, t) for t in seq_others])
    document_landings_own = net.keep(r.documents.at[xl], document_slot)
    upstream_landing = net.send(r.cotangent.at[1 - xl], r.upstream.at[xl], partner)
    upstream_own = net.keep(r.cotangent.at[xl], r.upstream.at[xl])

    forwarded = {}

    def block_of(dz, dx):
        return r.row.at[(z - dz) % ZS, (xl + dx) % 2, c]

    def to_sibling(dz, dx):
        forwarded[dz, dx] = net.send(block_of(dz, dx), block_of(dz, dx), sibling)

    def project(dz):
        source = (z - dz) % ZS
        for dx in range(2):
            forwarded[dz, dx].wait()
        rows = aligned(source, BLOCK)
        product = dot_nn(r.row[source].reshape(BLOCK, 1024), r.head_weights[...])
        r.raw[rows, :] = product[:, :384]
        r.values[rows, :] = product[:, 384:].astype(BF16)
        for part in range(3):
            gain = r.query_gain[...] if part < 2 else r.key_gain[...]
            normed, inverse = normalize(product[:, part * HD : (part + 1) * HD], gain)
            r.inverses[rows, part : part + 1] = inverse
            turned = normed * r.cosines[rows, :] + pltpu.roll(normed, 64, 1) * r.sines[rows, :]
            if part < 2:
                r.queries[rows, part * HD : (part + 1) * HD] = turned.astype(BF16)
            else:
                r.keys[rows, :] = turned.astype(BF16)

    loads = net.local_group()
    for ref, start, width in (
        (r.query_weight, 0, 256),
        (r.key_weight, 256, 128),
        (r.value_weight, 384, 128),
    ):
        loads.add(ref.at[:, aligned(head, width)], r.head_weights.at[:, pl.ds(start, width)])
    small_loads = net.local_group()
    small_loads.add(r.cosines_in, r.cosines).add(r.sines_in, r.sines)
    gain_loads = [
        net.keep(r.query_gain_in, r.query_gain),
        net.keep(r.key_gain_in, r.key_gain),
        net.keep(r.attention_gain_in, r.attention_gain),
        net.keep(r.feedforward_gain_in, r.feedforward_gain),
    ]
    load_wo = net.keep(r.output_weight, r.wo)
    load_wgu = net.keep(r.gate_weight, r.wgu.at[:, pl.ds(0, 3072)])
    load_wgu.add(r.up_weight, r.wgu.at[:, pl.ds(3072, 3072)])
    load_wd = net.keep(r.down_weight, r.wd)

    loads.wait()
    small_loads.wait()
    for load in gain_loads:
        load.wait()
    own_block.wait()
    to_sibling(0, 0)
    arrived[0, 1].wait()
    for dz, target in ((1, up_z), (3, down_z)):
        arrived[dz, 1] = net.send(block_of(0, 1), block_of(0, 1), target)
    to_sibling(0, 1)
    arrived[1, 0].wait()
    arrived[2, 0] = net.send(block_of(1, 0), block_of(1, 0), up_z)
    to_sibling(1, 0)
    arrived[3, 0].wait()
    to_sibling(3, 0)
    arrived[3, 1].wait()
    arrived[2, 1] = net.send(block_of(3, 1), block_of(3, 1), down_z)
    to_sibling(3, 1)
    arrived[1, 1].wait()
    to_sibling(1, 1)
    project(0)
    project(1)
    project(3)
    for dx in range(2):
        arrived[2, dx].wait()
        to_sibling(2, dx)
    document_landings.wait()
    document_landings_own.wait()
    lane = lax.broadcasted_iota(jnp.int32, (1, 128), 1)
    pieces = []
    for block in range(8):
        even = r.row_documents[2 * block, 0:1, :]
        odd = r.row_documents[2 * block + 1, 0:1, :]
        piece = jnp.where(lane < 64, even, odd)
        pieces.append(piece)
        r.document_column[block * 128 : (block + 1) * 128, :] = jnp.broadcast_to(piece, (128, 128)).T
    document_row = jnp.concatenate(pieces, axis=1)
    project(2)

    def visible_in(block):
        count = (block + 1) * BLOCK
        rows = slice(block * BLOCK, count)
        same = r.document_column[rows, 0:1] == document_row[:, :count]
        row_at = block * BLOCK + lax.broadcasted_iota(jnp.int32, (BLOCK, count), 0)
        column_at = lax.broadcasted_iota(jnp.int32, (BLOCK, count), 1)
        return same & (row_at >= column_at)

    attn_landings = {dz: [] for dz in ORDER}
    by_source = [[net.group() for _ in ORDER] for _ in range(2)]
    by_core = [net.local_group() for _ in range(2)]
    first_send, first_keep = by_source[0][0].index, by_core[0].index

    def head_copies(h):
        columns = aligned(h, HD)
        slot = r.attn_tokens.at[:, :, aligned(head * 2 + h, HD)]
        copies = [
            net.remote(r.attn_heads.at[t[2], :, t[4], :, columns], slot, t, first_send + h * 4 + dz)
            for (dz, _), t in zip(ZC, zc)
        ]
        own = pltpu.make_async_copy(
            r.attn_heads.at[z, :, c, :, columns], slot, net.local_sems.at[first_keep + h]
        )
        return copies + [own]

    @pl.loop(0, 2)
    def _(h):
        columns = aligned(h, HD)
        for block in range(4):
            rows = slice(block * BLOCK, (block + 1) * BLOCK)
            count = (block + 1) * BLOCK
            scores = dot_nt(r.queries[rows, columns], r.keys[:count, :])
            scores = jnp.where(visible_in(block), scores * (SCALE * LOG2E), MASKED)
            top = jnp.max(scores, axis=-1, keepdims=True)
            soft = jnp.exp2(scores - top)
            total = jnp.sum(soft, axis=-1, keepdims=True)
            mixed = dot_nn(soft.astype(BF16), r.values[:count, :]) / total
            r.attended[rows, columns] = mixed
            r.attn_heads[block, :, :, :, columns] = mixed.astype(BF16).reshape(2, 2, 64, HD)
            r.log_total[h, rows, :] = top + jnp.log2(total)
        for copy in head_copies(h):
            copy.start()

    for h in range(2):
        by_core[h].units = 2 * 64 * HD
        attn_landings[0].append(by_core[h])
        for dz in ORDER:
            by_source[h][dz].units = 2 * 64 * HD * (1 if dz == 0 else 2)
            attn_landings[dz].append(by_source[h][dz])

    def chain(shift, src, slot_of, half_of):
        ahead, behind = shift(1), shift(-1)
        state = Refs()
        state.slot_of, state.half_of, state.ahead, state.behind = slot_of, half_of, ahead, behind
        state.far = shift(2)
        state.from_behind = net.send(src, slot_of(at), ahead)
        state.from_ahead = net.send(src, slot_of(at), behind)
        state.near = [net.send(src, slot_of(at), sibling), net.keep(src, slot_of(at))]
        return state

    def chain_middle(state):
        half_of, behind, ahead = state.half_of, state.behind, state.ahead
        state.from_behind.wait()
        state.beyond = [net.send(half_of(behind, 0), half_of(behind, 0), ahead)]
        state.from_ahead.wait()
        state.beyond.append(net.send(half_of(ahead, 1), half_of(ahead, 1), behind))
        for source in (behind, ahead):
            state.near.append(net.send(state.slot_of(source), state.slot_of(source), sibling))

    def chain_forward(state):
        for landing in state.beyond:
            landing.wait()
        state.last = net.send(state.slot_of(state.far), state.slot_of(state.far), sibling)

    def chain_near(state):
        for item in state.near:
            item.wait()

    def chain_wait(state):
        chain_near(state)
        state.last.wait()

    load_wo.wait()
    turned = jnp.zeros((1024, 128), F32)
    for dz in ORDER:
        for landing in attn_landings[dz]:
            landing.wait()
        columns = aligned((z - dz) % ZS, 512)
        turned = turned + dot_nt(r.wo[:, columns], r.attn_tokens[:, :, columns].reshape(128, 512))
    branch = turned.T
    r.branch[...] = branch
    branch_normed, branch_inverse = normalize(branch, r.attention_gain[...])
    residual = r.row[z, :, c].reshape(128, 1024).astype(F32) + branch_normed
    r.residual[...] = residual
    r.residual_low[...] = residual.astype(BF16)
    def rows_of(group, index):
        def slot_of(who):
            return group.at[aligned(index(who) * 2 + who[4], 128), :]

        def half_of(who, half):
            return group.at[aligned((index(who) * 2 + who[4]) * 2 + half, 64), :]

        return (slot_of, half_of)

    def y_of(who):
        return who[1]

    def x_of(who):
        return who[0] * 2 + who[3]

    residual_chain = chain(lambda step: shifted(at, dy=step), r.residual_low, *rows_of(r.residual_y, y_of))
    load_wgu.wait()

    @pl.loop(0, 3)
    def _(tile):
        columns, up_columns = aligned(tile, 1024), aligned(tile + 3, 1024)
        gate = dot_nn(r.residual_low[...], r.wgu[:, columns])
        up = dot_nn(r.residual_low[...], r.wgu[:, up_columns])
        sigmoid_gate = lax.logistic(gate)
        silu = gate * sigmoid_gate
        r.activated[:, columns] = (silu * up).astype(BF16)
        r.up_factor[:, columns] = silu
        r.gate_factor[:, columns] = up * sigmoid_gate * (1.0 + gate * (1.0 - sigmoid_gate))

    def to_columns(src, first, group, index, targets):
        slot = group.at[aligned(index(at) * 2 + c, 128), :]
        items = net.together(
            [(src.at[:, aligned(first + index(t) * 2 + t[4], 384)], slot, t) for t in targets]
        )
        return [items, net.keep(src.at[:, aligned(first + index(at) * 2 + c, 384)], slot)]

    activated_landings = to_columns(r.activated, 0, r.activated_all, x_of, xc)
    load_wd.wait()

    @pl.loop(0, 2)
    def _(part):
        rows = aligned(part, 512)
        r.down[:, rows] = dot_nt(r.wd[rows, :], r.activated[...]).T

    down = r.down[...]
    upstream_landing.wait()
    upstream_own.wait()
    down_normed, down_inverse = normalize(down, r.feedforward_gain[...])
    layer_output = (r.residual[...] + down_normed).reshape(2, 64, 1024)
    r.layer_output[...] = layer_output
    r.out_low[...] = layer_output.astype(BF16)
    upstream = r.upstream[...].reshape(128, 1024).astype(F32)
    down_grad, feedforward_gain_grad = norm_back(upstream, down, down_inverse, r.feedforward_gain[...])
    r.down_low[...] = down_grad.astype(BF16)
    down_chain = chain(lambda step: shifted(at, dx=step), r.down_low, *rows_of(r.down_all, x_of))

    @pl.loop(0, 3)
    def _(tile):
        columns, up_columns = aligned(tile, 1024), aligned(tile + 3, 1024)
        act_grad = dot_nn(r.down_low[...], r.wd[:, columns])
        r.gate_up_low[:, columns] = (act_grad * r.gate_factor[:, columns]).astype(BF16)
        r.gate_up_low[:, up_columns] = (act_grad * r.up_factor[:, columns]).astype(BF16)

    up_landings = to_columns(r.gate_up_low, 8, r.up_all, y_of, yc)

    @pl.loop(0, 2)
    def _(part):
        rows = aligned(part, 512)
        r.residual_grad[:, rows] = dot_nt(r.wgu[rows, :], r.gate_up_low[...]).T

    chain_middle(residual_chain)
    residual_grad = r.upstream[...].reshape(128, 1024).astype(F32) + r.residual_grad[...]
    r.residual_grad[...] = residual_grad
    branch_grad, attention_gain_grad = norm_back(
        residual_grad, r.branch[...], branch_inverse, r.attention_gain[...]
    )
    for i in range(8):
        r.gains_own[i : i + 1, :] = attention_gain_grad[:, i * 128 : (i + 1) * 128]
        r.gains_own[8 + i : 9 + i, :] = feedforward_gain_grad[:, i * 128 : (i + 1) * 128]
    branch_low = branch_grad.astype(BF16)
    r.branch_low[...] = branch_low.reshape(2, 64, 1024)

    @pl.loop(0, 2)
    def _(tile):
        columns = aligned(tile, 1024)
        product = dot_nn(r.branch_low[...].reshape(128, 1024), r.wo[:, columns])
        r.attn_grad[:, :, columns] = product.astype(BF16).reshape(2, 64, 1024)

    attn_grad_landings = net.together(
        [(r.attn_grad.at[:, :, aligned(t[2] * 2 + t[4], 256)], r.attn_grad_row.at[z, :, c], t) for t in zc]
    )
    attn_grad_own = net.keep(r.attn_grad.at[:, :, aligned(head, 256)], r.attn_grad_row.at[z, :, c])
    branch_chain = chain(
        lambda step: shifted(at, dz=step),
        r.branch_low,
        lambda who: r.branch_row.at[who[2], :, who[4]],
        lambda who, half: r.branch_row.at[who[2], half, who[4]],
    )
    gate_landings = to_columns(r.gate_up_low, 0, r.gate_all, y_of, yc)
    head_loads = net.local_group()
    for i in range(8):
        for ref, start, width in (
            (r.query_weight, 0, 256),
            (r.key_weight, 256, 128),
            (r.value_weight, 384, 128),
        ):
            head_loads.add(ref.at[:, pl.ds(i * width, width)], r.wgu.at[:, pl.ds(i * 512 + start, width)])
    def total(own, others, landings):
        for landing in landings:
            landing.wait()
        result = own.astype(F32)
        for i in range(3):
            result = result + others[i].astype(F32)
        return result

    def wait_all(items):
        for item in items:
            item.wait()

    across = shifted(at, flip_xh=1)
    ending = net.group()
    ending_own = net.local_group()

    def replicate(src, slot_of, y_first):
        ending_own.add(src, slot_of(at))
        if y_first:
            along = [net.send(src, slot_of(at), t) for t in ys]
            ending.add(src, slot_of(at), across)
        else:
            over = net.send(src, slot_of(at), across)
            for t in ys:
                ending.add(src, slot_of(at), t)

        def second():
            if y_first:
                for step, landing in enumerate(along):
                    landing.wait()
                    source = shifted(at, dy=-(step + 1))
                    ending.add(slot_of(source), slot_of(source), across)
            else:
                over.wait()
                for t in ys:
                    ending.add(slot_of(across), slot_of(across), t)

        return second

    def along_y(src, slot):
        ending_own.add(src, slot)
        for t in ys:
            ending.add(src, slot, t)

    def swap(own, low, own_to, got_to):
        ending.add(low.at[1 - xl], got_to, partner)
        ending_own.add(own.at[xl], own_to)

    r.key_sum[...] = jnp.zeros_like(r.key_sum)
    r.value_sum[...] = jnp.zeros_like(r.value_sum)
    attn_grad_landings.wait()
    attn_grad_own.wait()

    def rope_norm_back(grad, part, rows, gain):
        turned = grad * r.cosines[rows, :] - pltpu.roll(grad, 64, 1) * r.sines[rows, :]
        vector = r.raw[rows, part * HD : (part + 1) * HD]
        result, gain_part = norm_back(turned, vector, r.inverses[rows, part : part + 1], gain)
        return (result.astype(BF16).reshape(2, 2, 64, HD), gain_part)

    def backward_block(block):
        rows = slice(block * BLOCK, (block + 1) * BLOCK)
        count = (block + 1) * BLOCK
        visible = visible_in(block)
        for h in range(2):
            columns = slice(h * HD, (h + 1) * HD)
            query = r.queries[rows, columns]
            grad = r.attn_grad_row[block, :, :, :, columns].reshape(BLOCK, HD)
            delta = jnp.sum(grad.astype(F32) * r.attended[rows, columns], axis=-1, keepdims=True)
            scores = dot_nt(query, r.keys[:count, :]) * (SCALE * LOG2E)
            soft = jnp.exp2(jnp.where(visible, scores - r.log_total[h, rows, :], MASKED))
            r.value_sum[:count, :] += dot_tn(soft.astype(BF16), grad)
            soft_grad = dot_nt(grad, r.values[:count, :])
            score_low = (soft * (soft_grad - delta)).astype(BF16)
            query_grad = dot_nn(score_low, r.keys[:count, :]) * SCALE
            r.key_sum[:count, :] += dot_tn(score_low, query)
            low, gain_part = rope_norm_back(query_grad, h, rows, r.query_gain[...])
            r.lows[block, :, :, :, columns] = low
            r.gains_own[16:17, :] += gain_part

    def by_rows(product):
        return product.astype(BF16).reshape(4, 2, 2, 2, 32, 384)

    def to_heads(done, got, width):
        items = [net.together([(done.at[t[2], t[4]], got.at[:, aligned(head, width)], t) for t in zc])]
        return items + [net.keep(done.at[z, c], got.at[:, aligned(head, width)])]

    r.gains_own[16:24, :] = jnp.zeros((8, 128), F32)
    wait_all(activated_landings)
    load_activated = net.keep(r.activated_all, r.wd.at[:, pl.ds(768, 384)])
    backward_block(0)
    chain_near(residual_chain)
    near_up = net.local_group()
    for who in (at, residual_chain.behind, residual_chain.ahead):
        rows = aligned(y_of(who), 256)
        near_up.add(r.residual_y.at[rows, :], r.wo.at[rows, pl.ds(0, 1024)])
    chain_forward(residual_chain)
    backward_block(1)
    chain_wait(residual_chain)
    rows = aligned(y_of(residual_chain.far), 256)
    far_up = net.keep(r.residual_y.at[rows, :], r.wo.at[rows, pl.ds(0, 1024)])
    backward_block(2)
    chain_middle(down_chain)
    wait_all(up_landings)
    load_up = net.keep(r.up_all, r.wd.at[:, pl.ds(0, 384)])
    backward_block(3)
    chain_middle(branch_chain)
    wait_all([near_up, far_up, load_up])
    r.own_up[...] = by_rows(dot_tn(r.wo[:, :1024], r.wd[:, :384]))
    first_up = [net.together([(r.own_up.at[:, t[3], :, t[0]], r.all_up.at[i], t) for i, t in enumerate(xs)])]
    key_total = jnp.zeros((1, HD), F32)
    for block in range(4):
        rows = slice(block * BLOCK, (block + 1) * BLOCK)
        low, gain_part = rope_norm_back(r.key_sum[rows, :] * SCALE, 2, rows, r.key_gain[...])
        r.lows[block, :, :, :, 256:384] = low
        r.lows[block, :, :, :, 384:] = r.value_sum[rows, :].astype(BF16).reshape(2, 2, 64, HD)
        key_total = key_total + gain_part
    r.gains_own[17:18, :] = key_total
    low_landings = {dz: net.group() for dz in ORDER}

    def send_lows(dz_here):
        for (dz, dc), t in zip(ZC, zc):
            if dz == dz_here:
                low_landings[dz].add(r.lows.at[t[2], :, t[4]], r.low_tokens.at[:, :, aligned(head, 512)], t)

    low_own = net.keep(r.lows.at[z, :, c], r.low_tokens.at[:, :, aligned(head, 512)])
    send_lows(0)
    gains_y = [net.together([(r.gains_own, r.gains_y.at[i], ys[i]) for i in range(3)])]
    send_lows(1)
    row = r.row[...].reshape(1024, 1024)
    low_columns = dot_tn(row, r.lows[...].reshape(1024, 512)).astype(BF16)
    r.own_query[...] = low_columns[:, :256].reshape(4, 2, 2, 4, 16, 256)
    first_query = [net.together([(r.own_query.at[:, :, :, t[1]], r.all_query.at[i], t) for i, t in enumerate(ys)])]
    r.own_kv[...] = low_columns[:, 256:].reshape(4, 2, 2, 4, 16, 256)
    first_kv = [net.together([(r.own_kv.at[:, t[3], :, :, :, aligned(t[0], 128)], r.all_kv.at[i], t) for i, t in enumerate(xs)])]
    wait_all(gate_landings)
    load_gate = net.keep(r.gate_all, r.wd.at[:, pl.ds(384, 384)])
    chain_near(down_chain)
    near_down = net.local_group()
    for who in (at, down_chain.behind, down_chain.ahead):
        rows = aligned(x_of(who), 256)
        near_down.add(r.down_all.at[rows, :], r.wgu.at[rows, pl.ds(4096, 1024)])
    chain_forward(down_chain)
    load_gate.wait()
    r.own_gate[...] = by_rows(dot_tn(r.wo[:, :1024], r.wd[:, 384:768]))
    first_gate = [net.together([(r.own_gate.at[t[2]], r.all_gate.at[i], t) for i, t in enumerate(zs)])]
    chain_wait(down_chain)
    rows = aligned(x_of(down_chain.far), 256)
    load_down = net.keep(r.down_all.at[rows, :], r.wgu.at[rows, pl.ds(4096, 1024)])
    wait_all([near_down, load_down, load_activated])
    product = dot_tn(r.wgu[:, 4096:5120], r.wd[:, 768:1152])
    r.own_down[...] = product.astype(BF16).reshape(4, 2, 2, 4, 16, 384)
    first_down = [net.together([(r.own_down.at[:, :, :, t[1]], r.all_down.at[i], t) for i, t in enumerate(ys)])]
    chain_forward(branch_chain)
    r.next_up[...] = total(r.own_up[:, at[3], :, at[0]], r.all_up, first_up).astype(BF16)
    then_up = [net.together([(r.next_up.at[t[2]], r.then_up.at[i], t) for i, t in enumerate(zs)])]
    r.gains_next[...] = total(r.gains_own[...], r.gains_y, gains_y)
    gains_x = [net.together([(r.gains_next, r.gains_x.at[i], xs[i]) for i in range(3)])]
    r.next_query[...] = total(r.own_query[:, :, :, at[1]], r.all_query, first_query).astype(BF16)
    then_query = [net.together([(r.next_query.at[:, t[3]], r.then_query.at[i], t) for i, t in enumerate(xs)])]
    chain_wait(branch_chain)
    output_columns = dot_tn(r.branch_row[...].reshape(1024, 1024), r.attn_heads[...].reshape(1024, 256))
    r.own_output[...] = output_columns.astype(BF16).reshape(4, 2, 2, 4, 16, 256)
    first_output = [net.together([(r.own_output.at[:, :, :, t[1]], r.all_output.at[i], t) for i, t in enumerate(ys)])]
    send_lows(3)
    r.next_kv[...] = total(r.own_kv[:, at[3], :, :, :, aligned(at[0], 128)], r.all_kv, first_kv).astype(BF16)
    then_kv = [net.together([(r.next_kv.at[:, :, t[1]], r.then_kv.at[i], t) for i, t in enumerate(ys)])]
    r.next_gate[...] = total(r.own_gate[at[2]], r.all_gate, first_gate).astype(BF16)
    then_gate = [net.together([(r.next_gate.at[t[3], :, t[0]], r.then_gate.at[i], t) for i, t in enumerate(xs)])]
    swap(r.layer_output, r.out_low, r.out_own, r.out_got)
    r.done_up[...] = total(r.next_up[z], r.then_up, then_up).astype(BF16)
    got_up = [
        net.send(r.done_up.at[1 - c], r.got_up.at[:, aligned(c, 384)], sibling),
        net.keep(r.done_up.at[c], r.got_up.at[:, aligned(c, 384)]),
    ]
    r.next_down[...] = total(r.own_down[:, :, :, at[1]], r.all_down, first_down).astype(BF16)
    then_down = [net.together([(r.next_down.at[t[2]], r.then_down.at[i], t) for i, t in enumerate(zs)])]
    r.gains_last[...] = total(r.gains_next[...], r.gains_x, gains_x)
    gains_zc = [net.together([(r.gains_last, r.gains_zc.at[i], t) for i, t in enumerate(zc)])]
    wait_all(got_up)
    second_up = replicate(r.got_up, lambda who: r.up_grad.at[aligned(who[0], 32), aligned(who[1], 768)], True)
    r.done_query[...] = total(r.next_query[:, xl], r.then_query, then_query).astype(BF16)
    got_query = to_heads(r.done_query, r.got_query, 256)
    send_lows(2)
    r.done_gate[...] = total(r.next_gate[xl, :, xh], r.then_gate, then_gate).astype(BF16)
    got_gate = [
        net.send(r.done_gate.at[1 - c], r.got_gate.at[:, aligned(c, 384)], sibling),
        net.keep(r.done_gate.at[c], r.got_gate.at[:, aligned(c, 384)]),
    ]
    r.done_down[...] = total(r.next_down[z], r.then_down, then_down).astype(BF16)
    quarter = aligned(xl * 2 + c, 384)
    pairs = [partner, shifted(at, flip_xl=1, dc=1), sibling]
    got_down = [net.together([(r.done_down.at[t[3], t[4]], r.got_down.at[:, quarter], t) for t in pairs])]
    got_down.append(net.keep(r.done_down.at[xl, c], r.got_down.at[:, quarter]))
    wait_all(got_gate)
    second_gate = replicate(r.got_gate, lambda who: r.gate_grad.at[aligned(who[0], 32), aligned(who[1], 768)], False)
    r.next_output[...] = total(r.own_output[:, :, :, at[1]], r.all_output, first_output).astype(BF16)
    then_output = [net.together([(r.next_output.at[:, t[3]], r.then_output.at[i], t) for i, t in enumerate(xs)])]
    r.done_kv[...] = total(r.next_kv[:, :, y], r.then_kv, then_kv).astype(BF16)
    got_kv = to_heads(r.done_kv, r.got_kv, 128)
    wait_all(got_query)
    along_y(r.got_query, r.query_weight_grad.at[aligned(y, 16), :])
    wait_all(got_down)
    second_down = replicate(r.got_down, lambda who: r.down_grad.at[aligned(who[1], 16), aligned(who[0], 1536)], True)
    second_gate()
    wait_all(got_kv)
    second_kv = replicate(r.got_kv, lambda who: r.key_value_grad.at[who[0], aligned(who[1], 16), :], False)
    second_up()
    head_loads.wait()
    low_own.wait()
    for dz in ORDER:
        low_landings[dz].wait()

    @pl.loop(0, 2)
    def _(part):
        rows = aligned(part, 512)
        r.down[:, rows] = dot_nt(r.wgu[rows, pl.ds(0, 4096)], r.low_tokens[...].reshape(128, 4096)).T

    input_grad = (r.residual_grad[...] + r.down[...]).reshape(2, 64, 1024)
    r.input_grad[...] = input_grad
    r.grad_low[...] = input_grad.astype(BF16)
    swap(r.input_grad, r.grad_low, r.grad_own, r.grad_got)
    r.done_output[...] = total(r.next_output[:, xl], r.then_output, then_output).astype(BF16)
    got_output = to_heads(r.done_output, r.got_output, 256)
    second_kv()
    second_down()
    wait_all(got_output)
    along_y(r.got_output, r.output_weight_grad.at[aligned(y, 16), :])
    wait_all(gains_zc)
    gains = r.gains_last[...]
    for i in range(7):
        gains = gains + r.gains_zc[i]
    r.gains_final[...] = gains
    net.keep(r.gains_final, r.gains)
    assert (net.next_send, net.next_keep) == (SENDS, KEEPS), (net.next_send, net.next_keep)
    net.drain()


def layer(*arrays):
    return pl.pallas_call(
        layer_kernel,
        out_shape=[shape(*item) for item in OUTPUTS.values()],
        in_specs=[pl.BlockSpec(memory_space=pl.ANY)] * len(INPUTS),
        out_specs=[pl.BlockSpec(memory_space=pl.ANY)] * len(OUTPUTS),
        scratch_shapes=[pltpu.VMEM(*item) for item in [*SCRATCH.values(), *SMALL.values()]]
        + [
            pltpu.SemaphoreType.DMA((SENDS,)),
            pltpu.SemaphoreType.DMA((SENDS,)),
            pltpu.SemaphoreType.DMA((KEEPS,)),
        ],
        compiler_params=pltpu.CompilerParams(
            collective_id=0, has_side_effects=True, vmem_limit_bytes=VMEM_LIMIT
        ),
        name="layer",
    )(*arrays)


def widen_kernel(
    out_own, grad_own, out_got, grad_got, query, key_value, output, gate, up, down, gains,
    out_to, grad_to, query_to, key_to, value_to, output_to, gate_to, up_to, down_to,
    query_gain, key_gain, attention_gain, feedforward_gain,
):
    lower = (lax.axis_index("seq") // 2) % 2 == 0
    for own, got, to in ((out_own, out_got, out_to), (grad_own, grad_got, grad_to)):
        mine, other = own[...], got[...].astype(F32)
        to[0] = jnp.where(lower, mine, other)
        to[1] = jnp.where(lower, other, mine)
    query_to[...] = query[...].astype(F32)
    key_to[...] = key_value[0].astype(F32)
    value_to[...] = key_value[1].astype(F32)
    output_to[...] = output[...].astype(F32)
    gate_to[...] = gate[...].astype(F32)
    up_to[...] = up[...].astype(F32)
    down_to[...] = down[...].astype(F32)
    attention_gain[...] = gains[0:8, :]
    feedforward_gain[...] = gains[8:16, :]
    query_gain[...] = gains[16:17, :]
    key_gain[...] = gains[17:18, :]


def widen(*arrays):
    steps = 2
    rows = 64 // steps

    def flat(columns):
        return pl.BlockSpec((rows, columns), lambda i: (i, 0))

    def paired(columns):
        return pl.BlockSpec((2, rows, columns), lambda i: (0, i, 0))

    def whole(count):
        return pl.BlockSpec((count, 128), lambda i: (0, 0))

    return pl.pallas_call(
        widen_kernel,
        grid=(steps,),
        out_shape=[shape((2, 64, 1024), F32)] * 2
        + [shape((64, n), F32) for n in (2048, 1024, 1024, 2048, 3072, 3072, 3072)]
        + [shape((n, 128), F32) for n in (1, 1, 8, 8)],
        in_specs=[flat(1024)] * 4
        + [flat(2048), paired(1024), flat(2048)]
        + [flat(3072)] * 3
        + [whole(24)],
        out_specs=[paired(1024)] * 2
        + [flat(n) for n in (2048, 1024, 1024, 2048, 3072, 3072, 3072)]
        + [whole(n) for n in (1, 1, 8, 8)],
        name="widen",
    )(*arrays)


VMEM_LIMIT = 63 * 2**20


def per_device(
    hidden_in,
    query_weight,
    key_weight,
    value_weight,
    output_weight,
    gate_weight,
    up_weight,
    down_weight,
    query_gain,
    key_gain,
    attention_gain,
    feedforward_gain,
    document_ids,
    cotangent,
):
    results = layer(
        hidden_in, cotangent,
        query_weight, key_weight, value_weight, output_weight, gate_weight, up_weight, down_weight,
        document_ids, *rope_tables(),
        query_gain[None, :], key_gain[None, :], attention_gain[None, :], feedforward_gain[None, :],
    )[:11]
    results = widen(*results)
    return tuple(results[:9]) + (results[9][0], results[10][0], results[11].reshape(1024), results[12].reshape(1024))


def solution(mesh):
    tokens = P("rows", "seq", None)
    split = P("seq", None)
    return jax.shard_map(
        per_device,
        mesh=mesh,
        in_specs=(tokens,) + (P(),) * 11 + (P("rows", "seq"), tokens),
        out_specs=(tokens, tokens) + (split,) * 7 + (P(),) * 4,
        check_vma=False,
    )
```

time: 156 us -> 122 us (0.78); the launches traced: 153 us -> 122 us
  Pallas kernels: 139 us -> 121 us
  other arithmetic: 9 us -> 0 us
  local copies, waits for them, and re-layouts: 4.77 us -> 0 us
    pallas_call x1 -> x2, Pallas kernels: 139 us -> 121 us  [the longest x1 117 us: layer(): pl.pallas_call(layer_kernel, out_shape=[shape(*item) for item in OUTPUTS....]
    convert_element_type x5 -> x0, other arithmetic: 8.92 us -> none  [the longest x1 2.41 us: per_device(): gate_up_grad[1].astype(F32)]
    unnamed x6 -> x0, local copies, waits for them, and re-layouts: 1.59 us -> none
where the time goes in v1:
time: 122 us
  Pallas kernels  121 us (99%)
    pallas_call x1, Pallas kernels, layer(): pl.pallas_call(layer_kernel, out_shape=[shape(*item) for item in OUTPUTS....  117 us
    pallas_call x1, Pallas kernels, widen(): pl.pallas_call(widen_kernel, grid=(steps,), out_shape=[shape((2, 64, 1024...  3.89 us

profile of v1, /device:TPU:1, one launch (start us, length us, event | category | flops | bytes accessed | tf_op | source)
XLA Modules:
  0.0 121.6 jit_solution(13351486906263865087)
XLA Ops:
  0.7 116.9 %layer.1 = (f32[64,1024]{1,0:T(8,128)}, f32[64,1024]{1,0:T(8,128)}, bf16[64,1024]{1,0:T(8,128)(2,1)}, bf16[64,1024]{1,0:T(8,128)(2,1)}, bf16[64,2048]{1,0:T(8,12...) custom-call(bf16[2,64,1024]{2,1,0:T(8,128)(2,1)} %refs_0_.1, ...), custom_call_target="tpu_custom_call" | custom-call | tf_op jit(solution)/shard_map/layer/pallas_call | solution.py:909
  117.5 3.9 %widen.1 = (f32[2,64,1024]{2,1,0:T(8,128)}, f32[2,64,1024]{2,1,0:T(8,128)}, f32[64,2048]{1,0:T(8,128)}, f32[64,1024]{1,0:T(8,128)}, f32[64,1024]{1,0:T(8,128)}, ...) custom-call(f32[64,1024]{1,0:T(8,128)} %get-tuple-element.37.out_own, ...), custom_call_target="tpu_custom_call" | custom-call | tf_op jit(solution)/shard_map/widen/pallas_call | solution.py:963

commit v2 on v1

--- a/solution.py
+++ b/solution.py
@@ -162,8 +162,8 @@
 ZC = [(dz, dc) for dz in range(ZS) for dc in range(2) if (dz, dc) != (0, 0)]
 ORDER = (0, 1, 3, 2)
 BLOCK = 256
-SENDS = 87
-KEEPS = 39
+SENDS = 91
+KEEPS = 36
 
 
 def rope_tables():
@@ -291,9 +291,10 @@
     next_gate=((2, 2, 2, 32, 384), BF16),
     then_gate=((3, 2, 32, 384), BF16),
     done_gate=((2, 32, 384), BF16),
-    got_gate=((32, 768), BF16),
     own_query=((4, 2, 2, 4, 16, 256), BF16),
-    all_query=((3, 4, 2, 2, 16, 256), BF16),
+    all_query=((2, 4, 2, 2, 16, 256), BF16),
+    far_query=((2, 2, 2, 2, 16, 256), BF16),
+    mid_query=((2, 2, 2, 2, 16, 256), BF16),
     next_query=((4, 2, 2, 16, 256), BF16),
     then_query=((3, 4, 2, 16, 256), BF16),
     done_query=((4, 2, 16, 256), BF16),
@@ -305,7 +306,9 @@
     done_kv=((4, 2, 16, 128), BF16),
     got_kv=((16, 1024), BF16),
     own_output=((4, 2, 2, 4, 16, 256), BF16),
-    all_output=((3, 4, 2, 2, 16, 256), BF16),
+    all_output=((2, 4, 2, 2, 16, 256), BF16),
+    far_output=((2, 2, 2, 2, 16, 256), BF16),
+    mid_output=((2, 2, 2, 2, 16, 256), BF16),
     next_output=((4, 2, 2, 16, 256), BF16),
     then_output=((3, 4, 2, 16, 256), BF16),
     done_output=((4, 2, 16, 256), BF16),
@@ -315,13 +318,13 @@
     next_up=((4, 2, 32, 384), BF16),
     then_up=((3, 2, 32, 384), BF16),
     done_up=((2, 32, 384), BF16),
-    got_up=((32, 768), BF16),
     own_down=((4, 2, 2, 4, 16, 384), BF16),
-    all_down=((3, 4, 2, 2, 16, 384), BF16),
+    all_down=((2, 4, 2, 2, 16, 384), BF16),
+    far_down=((2, 2, 2, 2, 16, 384), BF16),
+    mid_down=((2, 2, 2, 2, 16, 384), BF16),
     next_down=((4, 2, 2, 16, 384), BF16),
     then_down=((3, 2, 2, 16, 384), BF16),
     done_down=((2, 2, 16, 384), BF16),
-    got_down=((16, 1536), BF16),
     gains_own=((24, 128), F32),
     gains_next=((24, 128), F32),
     gains_last=((24, 128), F32),
@@ -361,7 +364,8 @@
         shifted(at, dy=dy, flip_xh=dx) for dy in range(YS) for dx in range(2) if (dy, dx) != (0, 0)
     ]
 
-    barrier_targets = list(seq_others) + yc[1:] + xc[1:] + replicas
+    crossed = [shifted(at, dy=dy, dc=dc, flip_xl=1) for dy in range(1, YS) for dc in range(2)]
+    barrier_targets = list(seq_others) + yc[1:] + xc[1:] + replicas + crossed
     documents_load = net.keep(r.document_ids_in, r.document_ids)
     net.barrier(barrier_targets)
     up_z, down_z = shifted(at, dz=1), shifted(at, dz=-1)
@@ -642,16 +646,16 @@
         r.gains_own[8 + i : 9 + i, :] = feedforward_gain_grad[:, i * 128 : (i + 1) * 128]
     branch_low = branch_grad.astype(BF16)
     r.branch_low[...] = branch_low.reshape(2, 64, 1024)
-
-    @pl.loop(0, 2)
-    def _(tile):
-        columns = aligned(tile, 1024)
+    attn_grad_landings = net.group()
+    for dz in (2, 1, 3, 0):
+        columns = aligned((z + dz) % ZS, 512)
         product = dot_nn(r.branch_low[...].reshape(128, 1024), r.wo[:, columns])
-        r.attn_grad[:, :, columns] = product.astype(BF16).reshape(2, 64, 1024)
-
-    attn_grad_landings = net.together(
-        [(r.attn_grad.at[:, :, aligned(t[2] * 2 + t[4], 256)], r.attn_grad_row.at[z, :, c], t) for t in zc]
-    )
+        r.attn_grad[:, :, columns] = product.astype(BF16).reshape(2, 64, 512)
+        for (step, _), t in zip(ZC, zc):
+            if step == dz:
+                attn_grad_landings.add(
+                    r.attn_grad.at[:, :, aligned(t[2] * 2 + t[4], 256)], r.attn_grad_row.at[z, :, c], t
+                )
     attn_grad_own = net.keep(r.attn_grad.at[:, :, aligned(head, 256)], r.attn_grad_row.at[z, :, c])
     branch_chain = chain(
         lambda step: shifted(at, dz=step),
@@ -672,7 +676,7 @@
         for landing in landings:
             landing.wait()
         result = own.astype(F32)
-        for i in range(3):
+        for i in range(others.shape[0]):
             result = result + others[i].astype(F32)
         return result
 
@@ -681,31 +685,82 @@
             item.wait()
 
     across = shifted(at, flip_xh=1)
-    ending = net.group()
+    ending, swaps = net.group(), net.group()
     ending_own = net.local_group()
 
-    def replicate(src, slot_of, y_first):
-        ending_own.add(src, slot_of(at))
-        if y_first:
-            along = [net.send(src, slot_of(at), t) for t in ys]
-            ending.add(src, slot_of(at), across)
-        else:
-            over = net.send(src, slot_of(at), across)
-            for t in ys:
-                ending.add(src, slot_of(at), t)
+    def replicate(pieces, slot_of, wide_of, y_first):
+        along = [net.group() if y_first else ending for _ in ys]
+        over = ending if y_first else net.group()
+        for src, (xl_to, c_to), mine in pieces:
+            if mine:
+                ending_own.add(src, slot_of(at))
+            else:
+                ending.add(src, slot_of(at), (xh, y, z, xl_to, c_to))
+            over.add(src, slot_of(at), (1 - xh, y, z, xl_to, c_to))
+            for group, t in zip(along, ys):
+                group.add(src, slot_of(at), (xh, t[1], z, xl_to, c_to))
 
         def second():
             if y_first:
-                for step, landing in enumerate(along):
-                    landing.wait()
+                for step, group in enumerate(along):
+                    group.wait()
                     source = shifted(at, dy=-(step + 1))
-                    ending.add(slot_of(source), slot_of(source), across)
+                    ending.add(wide_of(source), wide_of(source), across)
             else:
                 over.wait()
                 for t in ys:
-                    ending.add(slot_of(across), slot_of(across), t)
+                    ending.add(wide_of(across), wide_of(across), t)
 
         return second
+
+    def both_cores(done):
+        return [(done.at[c], (xl, c), True), (done.at[1 - c], (xl, 1 - c), False)]
+
+    def four_devices(done):
+        return [
+            (done.at[xl_to, c_to], (xl_to, c_to), (same_xl, same_c) == (True, True))
+            for xl_to, same_xl in ((xl, True), (1 - xl, False))
+            for c_to, same_c in ((c, True), (1 - c, False))
+        ]
+
+    def one_device(got):
+        return [(got, (xl, c), True)]
+
+    def ring_start(piece_of, far, landed, targets):
+        ahead, opposite, behind = targets
+        half = far.shape[1]
+        first, last = pl.ds(0, half), pl.ds(half, half)
+        state = Refs()
+        state.targets, state.far, state.landed = targets, far, landed
+        state.from_far = net.together(
+            [
+                (piece_of(opposite).at[first], far.at[0], ahead),
+                (piece_of(opposite).at[last], far.at[1], behind),
+            ]
+        )
+        state.near = net.together(
+            [
+                (piece_of(ahead).at[last], landed.at[0, last], ahead),
+                (piece_of(behind).at[first], landed.at[1, first], behind),
+            ]
+        )
+        state.wait = lambda: (state.near.wait(), state.summed.wait())
+        return [state]
+
+    def ring_middle(states, value_of, middle):
+        (state,) = states
+        ahead, _, behind = state.targets
+        half = state.far.shape[1]
+        first, last = pl.ds(0, half), pl.ds(half, half)
+        state.from_far.wait()
+        middle[0] = (value_of(ahead)[:half].astype(F32) + state.far[0].astype(F32)).astype(BF16)
+        middle[1] = (value_of(behind)[half:].astype(F32) + state.far[1].astype(F32)).astype(BF16)
+        state.summed = net.together(
+            [
+                (middle.at[0], state.landed.at[0, first], ahead),
+                (middle.at[1], state.landed.at[1, last], behind),
+            ]
+        )
 
     def along_y(src, slot):
         ending_own.add(src, slot)
@@ -713,7 +768,7 @@
             ending.add(src, slot, t)
 
     def swap(own, low, own_to, got_to):
-        ending.add(low.at[1 - xl], got_to, partner)
+        swaps.add(low.at[1 - xl], got_to, partner)
         ending_own.add(own.at[xl], own_to)
 
     r.key_sum[...] = jnp.zeros_like(r.key_sum)
@@ -758,6 +813,8 @@
     wait_all(activated_landings)
     load_activated = net.keep(r.activated_all, r.wd.at[:, pl.ds(768, 384)])
     backward_block(0)
+    chain_middle(down_chain)
+    swap(r.layer_output, r.out_low, r.out_own, r.out_got)
     chain_near(residual_chain)
     near_up = net.local_group()
     for who in (at, residual_chain.behind, residual_chain.ahead):
@@ -765,18 +822,23 @@
         near_up.add(r.residual_y.at[rows, :], r.wo.at[rows, pl.ds(0, 1024)])
     chain_forward(residual_chain)
     backward_block(1)
+    backward_block(2)
     chain_wait(residual_chain)
     rows = aligned(y_of(residual_chain.far), 256)
     far_up = net.keep(r.residual_y.at[rows, :], r.wo.at[rows, pl.ds(0, 1024)])
-    backward_block(2)
-    chain_middle(down_chain)
     wait_all(up_landings)
     load_up = net.keep(r.up_all, r.wd.at[:, pl.ds(0, 384)])
     backward_block(3)
-    chain_middle(branch_chain)
     wait_all([near_up, far_up, load_up])
     r.own_up[...] = by_rows(dot_tn(r.wo[:, :1024], r.wd[:, :384]))
     first_up = [net.together([(r.own_up.at[:, t[3], :, t[0]], r.all_up.at[i], t) for i, t in enumerate(xs)])]
+    chain_middle(branch_chain)
+    chain_near(down_chain)
+    near_down = net.local_group()
+    for who in (at, down_chain.behind, down_chain.ahead):
+        rows = aligned(x_of(who), 256)
+        near_down.add(r.down_all.at[rows, :], r.wgu.at[rows, pl.ds(4096, 1024)])
+    chain_forward(down_chain)
     key_total = jnp.zeros((1, HD), F32)
     for block in range(4):
         rows = slice(block * BLOCK, (block + 1) * BLOCK)
@@ -795,86 +857,91 @@
     low_own = net.keep(r.lows.at[z, :, c], r.low_tokens.at[:, :, aligned(head, 512)])
     send_lows(0)
     gains_y = [net.together([(r.gains_own, r.gains_y.at[i], ys[i]) for i in range(3)])]
-    send_lows(1)
     row = r.row[...].reshape(1024, 1024)
     low_columns = dot_tn(row, r.lows[...].reshape(1024, 512)).astype(BF16)
     r.own_query[...] = low_columns[:, :256].reshape(4, 2, 2, 4, 16, 256)
-    first_query = [net.together([(r.own_query.at[:, :, :, t[1]], r.all_query.at[i], t) for i, t in enumerate(ys)])]
+    first_query = ring_start(lambda t: r.own_query.at[:, :, :, t[1]], r.far_query, r.all_query, ys)
     r.own_kv[...] = low_columns[:, 256:].reshape(4, 2, 2, 4, 16, 256)
     first_kv = [net.together([(r.own_kv.at[:, t[3], :, :, :, aligned(t[0], 128)], r.all_kv.at[i], t) for i, t in enumerate(xs)])]
+    send_lows(1)
     wait_all(gate_landings)
     load_gate = net.keep(r.gate_all, r.wd.at[:, pl.ds(384, 384)])
-    chain_near(down_chain)
-    near_down = net.local_group()
-    for who in (at, down_chain.behind, down_chain.ahead):
-        rows = aligned(x_of(who), 256)
-        near_down.add(r.down_all.at[rows, :], r.wgu.at[rows, pl.ds(4096, 1024)])
-    chain_forward(down_chain)
-    load_gate.wait()
-    r.own_gate[...] = by_rows(dot_tn(r.wo[:, :1024], r.wd[:, 384:768]))
-    first_gate = [net.together([(r.own_gate.at[t[2]], r.all_gate.at[i], t) for i, t in enumerate(zs)])]
     chain_wait(down_chain)
     rows = aligned(x_of(down_chain.far), 256)
     load_down = net.keep(r.down_all.at[rows, :], r.wgu.at[rows, pl.ds(4096, 1024)])
     wait_all([near_down, load_down, load_activated])
     product = dot_tn(r.wgu[:, 4096:5120], r.wd[:, 768:1152])
     r.own_down[...] = product.astype(BF16).reshape(4, 2, 2, 4, 16, 384)
-    first_down = [net.together([(r.own_down.at[:, :, :, t[1]], r.all_down.at[i], t) for i, t in enumerate(ys)])]
+    first_down = ring_start(lambda t: r.own_down.at[:, :, :, t[1]], r.far_down, r.all_down, ys)
+    load_gate.wait()
+    r.own_gate[...] = by_rows(dot_tn(r.wo[:, :1024], r.wd[:, 384:768]))
+    first_gate = [net.together([(r.own_gate.at[t[2]], r.all_gate.at[i], t) for i, t in enumerate(zs)])]
     chain_forward(branch_chain)
+    ring_middle(first_query, lambda t: r.own_query[:, :, :, t[1]], r.mid_query)
+    ring_middle(first_down, lambda t: r.own_down[:, :, :, t[1]], r.mid_down)
+    chain_wait(branch_chain)
+    output_columns = dot_tn(r.branch_row[...].reshape(1024, 1024), r.attn_heads[...].reshape(1024, 256))
+    r.own_output[...] = output_columns.astype(BF16).reshape(4, 2, 2, 4, 16, 256)
+    first_output = ring_start(lambda t: r.own_output.at[:, :, :, t[1]], r.far_output, r.all_output, ys)
     r.next_up[...] = total(r.own_up[:, at[3], :, at[0]], r.all_up, first_up).astype(BF16)
     then_up = [net.together([(r.next_up.at[t[2]], r.then_up.at[i], t) for i, t in enumerate(zs)])]
     r.gains_next[...] = total(r.gains_own[...], r.gains_y, gains_y)
     gains_x = [net.together([(r.gains_next, r.gains_x.at[i], xs[i]) for i in range(3)])]
     r.next_query[...] = total(r.own_query[:, :, :, at[1]], r.all_query, first_query).astype(BF16)
     then_query = [net.together([(r.next_query.at[:, t[3]], r.then_query.at[i], t) for i, t in enumerate(xs)])]
-    chain_wait(branch_chain)
-    output_columns = dot_tn(r.branch_row[...].reshape(1024, 1024), r.attn_heads[...].reshape(1024, 256))
-    r.own_output[...] = output_columns.astype(BF16).reshape(4, 2, 2, 4, 16, 256)
-    first_output = [net.together([(r.own_output.at[:, :, :, t[1]], r.all_output.at[i], t) for i, t in enumerate(ys)])]
-    send_lows(3)
+    r.next_down[...] = total(r.own_down[:, :, :, at[1]], r.all_down, first_down).astype(BF16)
+    then_down = [net.together([(r.next_down.at[t[2]], r.then_down.at[i], t) for i, t in enumerate(zs)])]
     r.next_kv[...] = total(r.own_kv[:, at[3], :, :, :, aligned(at[0], 128)], r.all_kv, first_kv).astype(BF16)
     then_kv = [net.together([(r.next_kv.at[:, :, t[1]], r.then_kv.at[i], t) for i, t in enumerate(ys)])]
+    ring_middle(first_output, lambda t: r.own_output[:, :, :, t[1]], r.mid_output)
+    send_lows(3)
     r.next_gate[...] = total(r.own_gate[at[2]], r.all_gate, first_gate).astype(BF16)
     then_gate = [net.together([(r.next_gate.at[t[3], :, t[0]], r.then_gate.at[i], t) for i, t in enumerate(xs)])]
-    swap(r.layer_output, r.out_low, r.out_own, r.out_got)
-    r.done_up[...] = total(r.next_up[z], r.then_up, then_up).astype(BF16)
-    got_up = [
-        net.send(r.done_up.at[1 - c], r.got_up.at[:, aligned(c, 384)], sibling),
-        net.keep(r.done_up.at[c], r.got_up.at[:, aligned(c, 384)]),
-    ]
-    r.next_down[...] = total(r.own_down[:, :, :, at[1]], r.all_down, first_down).astype(BF16)
-    then_down = [net.together([(r.next_down.at[t[2]], r.then_down.at[i], t) for i, t in enumerate(zs)])]
     r.gains_last[...] = total(r.gains_next[...], r.gains_x, gains_x)
     gains_zc = [net.together([(r.gains_last, r.gains_zc.at[i], t) for i, t in enumerate(zc)])]
-    wait_all(got_up)
-    second_up = replicate(r.got_up, lambda who: r.up_grad.at[aligned(who[0], 32), aligned(who[1], 768)], True)
+    r.done_up[...] = total(r.next_up[z], r.then_up, then_up).astype(BF16)
+    second_up = replicate(
+        both_cores(r.done_up),
+        lambda who: r.up_grad.at[aligned(who[0], 32), aligned(who[1] * 2 + who[4], 384)],
+        lambda who: r.up_grad.at[aligned(who[0], 32), aligned(who[1], 768)],
+        True,
+    )
+    r.done_kv[...] = total(r.next_kv[:, :, y], r.then_kv, then_kv).astype(BF16)
+    got_kv = to_heads(r.done_kv, r.got_kv, 128)
+    r.done_down[...] = total(r.next_down[z], r.then_down, then_down).astype(BF16)
+    second_down = replicate(
+        four_devices(r.done_down),
+        lambda who: r.down_grad.at[aligned(who[1], 16), aligned((who[0] * 2 + who[3]) * 2 + who[4], 384)],
+        lambda who: r.down_grad.at[aligned(who[1], 16), aligned(who[0], 1536)],
+        False,
+    )
+    r.next_output[...] = total(r.own_output[:, :, :, at[1]], r.all_output, first_output).astype(BF16)
+    then_output = [net.together([(r.next_output.at[:, t[3]], r.then_output.at[i], t) for i, t in enumerate(xs)])]
     r.done_query[...] = total(r.next_query[:, xl], r.then_query, then_query).astype(BF16)
     got_query = to_heads(r.done_query, r.got_query, 256)
     send_lows(2)
     r.done_gate[...] = total(r.next_gate[xl, :, xh], r.then_gate, then_gate).astype(BF16)
-    got_gate = [
-        net.send(r.done_gate.at[1 - c], r.got_gate.at[:, aligned(c, 384)], sibling),
-        net.keep(r.done_gate.at[c], r.got_gate.at[:, aligned(c, 384)]),
-    ]
-    r.done_down[...] = total(r.next_down[z], r.then_down, then_down).astype(BF16)
-    quarter = aligned(xl * 2 + c, 384)
-    pairs = [partner, shifted(at, flip_xl=1, dc=1), sibling]
-    got_down = [net.together([(r.done_down.at[t[3], t[4]], r.got_down.at[:, quarter], t) for t in pairs])]
-    got_down.append(net.keep(r.done_down.at[xl, c], r.got_down.at[:, quarter]))
-    wait_all(got_gate)
-    second_gate = replicate(r.got_gate, lambda who: r.gate_grad.at[aligned(who[0], 32), aligned(who[1], 768)], False)
-    r.next_output[...] = total(r.own_output[:, :, :, at[1]], r.all_output, first_output).astype(BF16)
-    then_output = [net.together([(r.next_output.at[:, t[3]], r.then_output.at[i], t) for i, t in enumerate(xs)])]
-    r.done_kv[...] = total(r.next_kv[:, :, y], r.then_kv, then_kv).astype(BF16)
-    got_kv = to_heads(r.done_kv, r.got_kv, 128)
+    second_gate = replicate(
+        both_cores(r.done_gate),
+        lambda who: r.gate_grad.at[aligned(who[0], 32), aligned(who[1] * 2 + who[4], 384)],
+        lambda who: r.gate_grad.at[aligned(who[0], 32), aligned(who[1], 768)],
+        True,
+    )
+    wait_all(got_kv)
+    second_kv = replicate(
+        one_device(r.got_kv),
+        lambda who: r.key_value_grad.at[who[0], aligned(who[1], 16), :],
+        lambda who: r.key_value_grad.at[who[0], aligned(who[1], 16), :],
+        False,
+    )
+    second_down()
+    second_up()
+    r.done_output[...] = total(r.next_output[:, xl], r.then_output, then_output).astype(BF16)
+    got_output = to_heads(r.done_output, r.got_output, 256)
     wait_all(got_query)
     along_y(r.got_query, r.query_weight_grad.at[aligned(y, 16), :])
-    wait_all(got_down)
-    second_down = replicate(r.got_down, lambda who: r.down_grad.at[aligned(who[1], 16), aligned(who[0], 1536)], True)
     second_gate()
-    wait_all(got_kv)
-    second_kv = replicate(r.got_kv, lambda who: r.key_value_grad.at[who[0], aligned(who[1], 16), :], False)
-    second_up()
+    second_kv()
     head_loads.wait()
     low_own.wait()
     for dz in ORDER:
@@ -889,10 +956,6 @@
     r.input_grad[...] = input_grad
     r.grad_low[...] = input_grad.astype(BF16)
     swap(r.input_grad, r.grad_low, r.grad_own, r.grad_got)
-    r.done_output[...] = total(r.next_output[:, xl], r.then_output, then_output).astype(BF16)
-    got_output = to_heads(r.done_output, r.got_output, 256)
-    second_kv()
-    second_down()
     wait_all(got_output)
     along_y(r.got_output, r.output_weight_grad.at[aligned(y, 16), :])
     wait_all(gains_zc)

time: 122 us -> 116 us (0.951); the launches traced: 122 us -> 114 us
  Pallas kernels: 121 us -> 113 us
    pallas_call x1, Pallas kernels: 117 us -> 109 us  [layer(): pl.pallas_call(layer_kernel, out_shape=[shape(*item) for item in OUTPUTS....]
where the time goes in v2:
time: 116 us; the launch traced here: 114 us
  Pallas kernels  113 us (97%)
    pallas_call x1, Pallas kernels, layer(): pl.pallas_call(layer_kernel, out_shape=[shape(*item) for item in OUTPUTS....  109 us
    pallas_call x1, Pallas kernels, widen(): pl.pallas_call(widen_kernel, grid=(steps,), out_shape=[shape((2, 64, 1024...  3.89 us

profile of v2, /device:TPU:1, one launch (start us, length us, event | category | flops | bytes accessed | tf_op | source)
XLA Modules:
  0.0 114.0 jit_solution(16090160874991681496)
XLA Ops:
  0.7 109.2 %layer.1 = (f32[64,1024]{1,0:T(8,128)}, f32[64,1024]{1,0:T(8,128)}, bf16[64,1024]{1,0:T(8,128)(2,1)}, bf16[64,1024]{1,0:T(8,128)(2,1)}, bf16[64,2048]{1,0:T(8,12...) custom-call(bf16[2,64,1024]{2,1,0:T(8,128)(2,1)} %refs_0_.1, ...), custom_call_target="tpu_custom_call" | custom-call | tf_op jit(solution)/shard_map/layer/pallas_call | solution.py:972
  109.9 3.9 %widen.1 = (f32[2,64,1024]{2,1,0:T(8,128)}, f32[2,64,1024]{2,1,0:T(8,128)}, f32[64,2048]{1,0:T(8,128)}, f32[64,1024]{1,0:T(8,128)}, f32[64,1024]{1,0:T(8,128)}, ...) custom-call(f32[64,1024]{1,0:T(8,128)} %get-tuple-element.37.out_own, ...), custom_call_target="tpu_custom_call" | custom-call | tf_op jit(solution)/shard_map/widen/pallas_call | solution.py:1026

commit v3 on v2

--- a/solution.py
+++ b/solution.py
@@ -48,11 +48,11 @@
 
 class Group:
     def __init__(self, net, index):
-        self.net, self.index = net, index
+        self.net, self.index, self.sender = net, index, index // BUCKET
         self.units, self.here = 0, False
 
     def add(self, src, dst, target, start=True):
-        copy = self.net.remote(src, dst, target, self.index)
+        copy = self.net.remote(src, dst, target, self.sender, self.index)
         if start:
             copy.start()
         self.units += units_of(dst)
@@ -62,10 +62,6 @@
         if not self.here:
             self.net.sized(self.units, self.net.recv_sems.at[self.index]).wait()
             self.here = True
-
-    def drain(self):
-        self.wait()
-        self.net.sized(self.units, self.net.send_sems.at[self.index]).wait()
 
 
 class LocalGroup:
@@ -116,11 +112,11 @@
             pl.semaphore_signal(barrier, inc=1, device_id=device(*target), device_id_type=MESH)
         pl.semaphore_wait(barrier, len(targets))
 
-    def remote(self, src, dst, target, i):
+    def remote(self, src, dst, target, sender, i):
         return pltpu.make_async_remote_copy(
             src_ref=src,
             dst_ref=dst,
-            send_sem=self.send_sems.at[i],
+            send_sem=self.send_sems.at[sender],
             recv_sem=self.recv_sems.at[i],
             device_id=device(*target),
             device_id_type=MESH,
@@ -151,8 +147,12 @@
     def drain(self):
         for group in self.locals:
             group.wait()
+        sent = {}
         for group in self.groups:
-            group.drain()
+            group.wait()
+            sent[group.sender] = sent.get(group.sender, 0) + group.units
+        for sender, units in sent.items():
+            self.sized(units, self.send_sems.at[sender]).wait()
 
 
 def shape(dims, dtype=BF16):
@@ -162,7 +162,8 @@
 ZC = [(dz, dc) for dz in range(ZS) for dc in range(2) if (dz, dc) != (0, 0)]
 ORDER = (0, 1, 3, 2)
 BLOCK = 256
-SENDS = 91
+BUCKET = 15
+SENDS = 93
 KEEPS = 36
 
 
@@ -369,10 +370,13 @@
     documents_load = net.keep(r.document_ids_in, r.document_ids)
     net.barrier(barrier_targets)
     up_z, down_z = shifted(at, dz=1), shifted(at, dz=-1)
-    arrived = {}
-    arrived[0, 1] = net.send(r.hidden.at[1 - xl], r.row.at[z, xl, c], partner)
+    parts = [pl.ds(0, 32), pl.ds(32, 32)]
+    arrived = {(dz, dx): net.group() for dz, dx in ((1, 0), (3, 0), (1, 1))}
+    from_partner = [
+        net.send(r.hidden.at[1 - xl, part], r.row.at[z, xl, c, part], partner) for part in parts
+    ]
     for dz, target in ((1, up_z), (3, down_z)):
-        arrived[dz, 0] = net.send(r.hidden.at[xl], r.row.at[z, xl, c], target)
+        arrived[dz, 0].add(r.hidden.at[xl], r.row.at[z, xl, c], target)
     own_block = net.keep(r.hidden.at[xl], r.row.at[z, xl, c])
     documents_load.wait()
     own_documents = r.document_ids[...].astype(F32)
@@ -437,17 +441,23 @@
         load.wait()
     own_block.wait()
     to_sibling(0, 0)
-    arrived[0, 1].wait()
-    for dz, target in ((1, up_z), (3, down_z)):
-        arrived[dz, 1] = net.send(block_of(0, 1), block_of(0, 1), target)
+    below = [net.group() for _ in parts]
+    for landing, part, second in zip(from_partner, parts, below):
+        landing.wait()
+        piece = r.row.at[z, 1 - xl, c, part]
+        arrived[1, 1].add(piece, piece, up_z)
+        second.add(piece, piece, down_z)
     to_sibling(0, 1)
     arrived[1, 0].wait()
     arrived[2, 0] = net.send(block_of(1, 0), block_of(1, 0), up_z)
     to_sibling(1, 0)
     arrived[3, 0].wait()
     to_sibling(3, 0)
-    arrived[3, 1].wait()
-    arrived[2, 1] = net.send(block_of(3, 1), block_of(3, 1), down_z)
+    arrived[2, 1] = net.group()
+    for landing, part in zip(below, parts):
+        landing.wait()
+        piece = r.row.at[(z + 1) % ZS, 1 - xl, c, part]
+        arrived[2, 1].add(piece, piece, down_z)
     to_sibling(3, 1)
     arrived[1, 1].wait()
     to_sibling(1, 1)
@@ -480,6 +490,10 @@
 
     attn_landings = {dz: [] for dz in ORDER}
     by_source = [[net.group() for _ in ORDER] for _ in range(2)]
+    sender = by_source[0][0].sender
+    for groups in by_source:
+        for group in groups:
+            group.sender = sender
     by_core = [net.local_group() for _ in range(2)]
     first_send, first_keep = by_source[0][0].index, by_core[0].index
 
@@ -487,7 +501,7 @@
         columns = aligned(h, HD)
         slot = r.attn_tokens.at[:, :, aligned(head * 2 + h, HD)]
         copies = [
-            net.remote(r.attn_heads.at[t[2], :, t[4], :, columns], slot, t, first_send + h * 4 + dz)
+            net.remote(r.attn_heads.at[t[2], :, t[4], :, columns], slot, t, sender, first_send + h * 4 + dz)
             for (dz, _), t in zip(ZC, zc)
         ]
         own = pltpu.make_async_copy(
@@ -976,7 +990,7 @@
         out_specs=[pl.BlockSpec(memory_space=pl.ANY)] * len(OUTPUTS),
         scratch_shapes=[pltpu.VMEM(*item) for item in [*SCRATCH.values(), *SMALL.values()]]
         + [
-            pltpu.SemaphoreType.DMA((SENDS,)),
+            pltpu.SemaphoreType.DMA((-(-SENDS // BUCKET),)),
             pltpu.SemaphoreType.DMA((SENDS,)),
             pltpu.SemaphoreType.DMA((KEEPS,)),
         ],

time: 116 us -> 110 us (0.948); the launches traced: 114 us -> 110 us
  Pallas kernels: 113 us -> 109 us
    pallas_call x1, Pallas kernels: 109 us -> 105 us  [layer(): pl.pallas_call(layer_kernel, out_shape=[shape(*item) for item in OUTPUTS....]
where the time goes in v3:
time: 110 us
  Pallas kernels  109 us (99%)
    pallas_call x1, Pallas kernels, layer(): pl.pallas_call(layer_kernel, out_shape=[shape(*item) for item in OUTPUTS....  105 us
    pallas_call x1, Pallas kernels, widen(): pl.pallas_call(widen_kernel, grid=(steps,), out_shape=[shape((2, 64, 1024...  3.89 us

profile of v3, /device:TPU:1, one launch (start us, length us, event | category | flops | bytes accessed | tf_op | source)
XLA Modules:
  0.0 109.5 jit_solution(13185288294465720266)
XLA Ops:
  0.7 104.8 %layer.1 = (f32[64,1024]{1,0:T(8,128)}, f32[64,1024]{1,0:T(8,128)}, bf16[64,1024]{1,0:T(8,128)(2,1)}, bf16[64,1024]{1,0:T(8,128)(2,1)}, bf16[64,2048]{1,0:T(8,12...) custom-call(bf16[2,64,1024]{2,1,0:T(8,128)(2,1)} %refs_0_.1, ...), custom_call_target="tpu_custom_call" | custom-call | tf_op jit(solution)/shard_map/layer/pallas_call | solution.py:986
  105.5 3.9 %widen.1 = (f32[2,64,1024]{2,1,0:T(8,128)}, f32[2,64,1024]{2,1,0:T(8,128)}, f32[64,2048]{1,0:T(8,128)}, f32[64,1024]{1,0:T(8,128)}, f32[64,1024]{1,0:T(8,128)}, ...) custom-call(f32[64,1024]{1,0:T(8,128)} %get-tuple-element.37.out_own, ...), custom_call_target="tpu_custom_call" | custom-call | tf_op jit(solution)/shard_map/widen/pallas_call | solution.py:1040

commit v4 on v3

--- a/solution.py
+++ b/solution.py
@@ -48,7 +48,7 @@
 
 class Group:
     def __init__(self, net, index):
-        self.net, self.index, self.sender = net, index, index // BUCKET
+        self.net, self.index, self.sender = net, index, sum(index >= start for start in BUCKETS)
         self.units, self.here = 0, False
 
     def add(self, src, dst, target, start=True):
@@ -162,7 +162,7 @@
 ZC = [(dz, dc) for dz in range(ZS) for dc in range(2) if (dz, dc) != (0, 0)]
 ORDER = (0, 1, 3, 2)
 BLOCK = 256
-BUCKET = 15
+BUCKETS = (53,)
 SENDS = 93
 KEEPS = 36
 
@@ -950,23 +950,30 @@
     )
     second_down()
     second_up()
+    head_loads.wait()
+    low_own.wait()
+    for dz in (0, 1, 3):
+        low_landings[dz].wait()
+
+    @pl.loop(0, 2)
+    def _(part):
+        rows = aligned(part, 512)
+        turned = jnp.zeros((512, 128), F32)
+        for dz in (0, 1, 3):
+            columns = aligned((z - dz) % ZS, 1024)
+            turned = turned + dot_nt(r.wgu[rows, columns], r.low_tokens[:, :, columns].reshape(128, 1024))
+        r.down[:, rows] = turned.T
+
     r.done_output[...] = total(r.next_output[:, xl], r.then_output, then_output).astype(BF16)
     got_output = to_heads(r.done_output, r.got_output, 256)
     wait_all(got_query)
     along_y(r.got_query, r.query_weight_grad.at[aligned(y, 16), :])
     second_gate()
     second_kv()
-    head_loads.wait()
-    low_own.wait()
-    for dz in ORDER:
-        low_landings[dz].wait()
-
-    @pl.loop(0, 2)
-    def _(part):
-        rows = aligned(part, 512)
-        r.down[:, rows] = dot_nt(r.wgu[rows, pl.ds(0, 4096)], r.low_tokens[...].reshape(128, 4096)).T
-
-    input_grad = (r.residual_grad[...] + r.down[...]).reshape(2, 64, 1024)
+    low_landings[2].wait()
+    columns = aligned((z - 2) % ZS, 1024)
+    turned = dot_nt(r.wgu[:, columns], r.low_tokens[:, :, columns].reshape(128, 1024))
+    input_grad = (r.residual_grad[...] + r.down[...] + turned.T).reshape(2, 64, 1024)
     r.input_grad[...] = input_grad
     r.grad_low[...] = input_grad.astype(BF16)
     swap(r.input_grad, r.grad_low, r.grad_own, r.grad_got)
@@ -990,7 +997,7 @@
         out_specs=[pl.BlockSpec(memory_space=pl.ANY)] * len(OUTPUTS),
         scratch_shapes=[pltpu.VMEM(*item) for item in [*SCRATCH.values(), *SMALL.values()]]
         + [
-            pltpu.SemaphoreType.DMA((-(-SENDS // BUCKET),)),
+            pltpu.SemaphoreType.DMA((len(BUCKETS) + 1,)),
             pltpu.SemaphoreType.DMA((SENDS,)),
             pltpu.SemaphoreType.DMA((KEEPS,)),
         ],

time: 110 us -> 110 us (level)
  no operation moved by 1% of the time
where the time goes in v4:
time: 110 us
  Pallas kernels  109 us (99%)
    pallas_call x1, Pallas kernels, layer(): pl.pallas_call(layer_kernel, out_shape=[shape(*item) for item in OUTPUTS....  105 us
    pallas_call x1, Pallas kernels, widen(): pl.pallas_call(widen_kernel, grid=(steps,), out_shape=[shape((2, 64, 1024...  3.89 us

profile of v4, /device:TPU:1, one launch (start us, length us, event | category | flops | bytes accessed | tf_op | source)
XLA Modules:
  0.0 109.6 jit_solution(8996549546444210986)
XLA Ops:
  0.7 104.9 %layer.1 = (f32[64,1024]{1,0:T(8,128)}, f32[64,1024]{1,0:T(8,128)}, bf16[64,1024]{1,0:T(8,128)(2,1)}, bf16[64,1024]{1,0:T(8,128)(2,1)}, bf16[64,2048]{1,0:T(8,12...) custom-call(bf16[2,64,1024]{2,1,0:T(8,128)(2,1)} %refs_0_.1, ...), custom_call_target="tpu_custom_call" | custom-call | tf_op jit(solution)/shard_map/layer/pallas_call | solution.py:993
  105.5 3.9 %widen.1 = (f32[2,64,1024]{2,1,0:T(8,128)}, f32[2,64,1024]{2,1,0:T(8,128)}, f32[64,2048]{1,0:T(8,128)}, f32[64,1024]{1,0:T(8,128)}, f32[64,1024]{1,0:T(8,128)}, ...) custom-call(f32[64,1024]{1,0:T(8,128)} %get-tuple-element.37.out_own, ...), custom_call_target="tpu_custom_call" | custom-call | tf_op jit(solution)/shard_map/widen/pallas_call | solution.py:1047
